TPU v7x, 32 devices: a whole 2x2x4 slice. The times are simulated.
32 devices in a mesh: expert: 8 (over z, x), split: 2 (over y), replica: 2 (over core).
Axes of the slice: x: 2, y: 2, z: 4, core: 2. Of those that a mesh axis runs over, the one named last changes fastest.
Arguments:
- tokens: bfloat16 [2, 2048, 2048], P('replica', 'expert', 'split'), may hold values from -6 to 6
- grad_out: bfloat16 [2, 2048, 2048], P('replica', 'expert', 'split'), may hold values from -6 to 6
- expert_ids: int32 [2, 2048, 2], P('replica', 'expert'), may hold values from 0 to 7, all different within a row; in each aligned block of 256 rows (0 to 255, 256 to 511, ..., all dimensions but the last counted through in order) at most 128 rows name the same one
- route_probs: float32 [2, 2048, 2], P('replica', 'expert'), may hold values from 0.1 to 0.9
- w_gate: bfloat16 [2, 8, 2048, 512], P('replica', 'expert', None, 'split'), may hold values from -0.125 to 0.125
- w_up: bfloat16 [2, 8, 2048, 512], P('replica', 'expert', None, 'split'), may hold values from -0.125 to 0.125
- w_down: bfloat16 [2, 8, 512, 2048], P('replica', 'expert', 'split'), may hold values from -0.25 to 0.25
- mom_gate: bfloat16 [2, 8, 2048, 512], P('replica', 'expert', None, 'split'), may hold values from -24 to 24
- mom_up: bfloat16 [2, 8, 2048, 512], P('replica', 'expert', None, 'split'), may hold values from -24 to 24
Outputs:
- avg_gate_w: bfloat16 [8, 2048, 512], P('expert', None, 'split')
- avg_up_w: bfloat16 [8, 2048, 512], P('expert', None, 'split')
- avg_gate_m: bfloat16 [8, 2048, 512], P('expert', None, 'split')
- avg_up_m: bfloat16 [8, 2048, 512], P('expert', None, 'split')
- d_tokens: bfloat16 [2, 2048, 2048], P('replica', 'expert', 'split')
Inputs may be any that keep to these rules, and one draw needn't show every extreme that they name: `expert_ids`: each token names two different experts; among the 256 tokens of one device no expert is named more than 128 times, a bound that some block reaches on some device in every draw.
All inputs are finite; a program needn't handle non-finite values.
Results may differ from a plain program's by a relative error of at most 0.0065.
Values may be sent and summed in bfloat16 or wider, within the bound.
A program may use at most 128 MiB of HBM per device.

v0:
```python
import jax
import jax.numpy as jnp
from jax import lax
from jax.sharding import PartitionSpec as P

momentum_decay = 0.9
step_size = 0.005


def slot_targets(ids_block, experts, capacity):
    flat_ids = ids_block.reshape(-1)
    onehot = (flat_ids[:, None] == jnp.arange(experts, dtype=jnp.int32)[None, :]).astype(jnp.int32)
    slot_rank = jnp.sum((jnp.cumsum(onehot, axis=0) - 1) * onehot, axis=1)
    return flat_ids * capacity + slot_rank


def hidden_grads(rows_in, rows_out, gate_w, up_w, down_w):
    gate_pre = jnp.dot(rows_in, gate_w, preferred_element_type=jnp.float32)
    up_pre = jnp.dot(rows_in, up_w, preferred_element_type=jnp.float32)
    sigmoid_gate = jax.nn.sigmoid(gate_pre)
    activated = gate_pre * sigmoid_gate
    hidden_grad = lax.dot_general(
        rows_out, down_w, (((1,), (1,)), ((), ())), preferred_element_type=jnp.float32
    )
    d_up = (hidden_grad * activated).astype(jnp.bfloat16)
    d_gate = (hidden_grad * up_pre * sigmoid_gate * (1.0 + gate_pre * (1.0 - sigmoid_gate))).astype(
        jnp.bfloat16
    )
    g_gate = lax.dot_general(
        rows_in, d_gate, (((0,), (0,)), ((), ())), preferred_element_type=jnp.float32
    )
    g_up = lax.dot_general(
        rows_in, d_up, (((0,), (0,)), ((), ())), preferred_element_type=jnp.float32
    )
    return (g_gate, g_up, d_gate, d_up)


def back_rows(d_gate, d_up, gate_w, up_w):
    result = lax.dot_general(
        d_gate, gate_w, (((1,), (1,)), ((), ())), preferred_element_type=jnp.float32
    )
    return result + lax.dot_general(
        d_up, up_w, (((1,), (1,)), ((), ())), preferred_element_type=jnp.float32
    )


def per_device(tokens, grad_out, expert_ids, route_probs, w_gate, w_up, w_down, mom_gate, mom_up):
    experts = lax.axis_size("expert")
    tok_count = tokens.shape[1]
    capacity = 4 * tok_count // experts
    targets = slot_targets(expert_ids[0], experts, capacity)
    weights_route = route_probs[0]
    rows_in = tokens[0]
    feat_width = rows_in.shape[1]
    scaled = (grad_out[0][:, None, :].astype(jnp.float32) * weights_route[:, :, None]).astype(
        jnp.bfloat16
    )
    scaled = scaled.reshape(2 * tok_count, feat_width)
    repeated = jnp.repeat(rows_in, 2, axis=0)
    blank_rows = jnp.zeros((experts * capacity, feat_width), jnp.bfloat16)
    slots_in = blank_rows.at[targets].set(repeated).reshape(experts, capacity, feat_width)
    slots_out = blank_rows.at[targets].set(scaled).reshape(experts, capacity, feat_width)
    half_in, half_out = (
        lax.all_to_all(slots_in, "expert", split_axis=0, concat_axis=0, tiled=True),
        lax.all_to_all(slots_out, "expert", split_axis=0, concat_axis=0, tiled=True),
    )
    recv_in, recv_out = (
        lax.all_gather(half_in, "split", axis=2, tiled=True),
        lax.all_gather(half_out, "split", axis=2, tiled=True),
    )
    row_count = recv_in.shape[0] * recv_in.shape[1]
    full_width = recv_in.shape[2]
    gate_local = w_gate[0, 0]
    up_local = w_up[0, 0]
    g_gate, g_up, d_gate, d_up = hidden_grads(
        recv_in.reshape(row_count, full_width),
        recv_out.reshape(row_count, full_width),
        gate_local,
        up_local,
        w_down[0, 0],
    )
    m_gate = momentum_decay * mom_gate[0, 0].astype(jnp.float32) + g_gate
    m_up = momentum_decay * mom_up[0, 0].astype(jnp.float32) + g_up
    new_gate = (gate_local.astype(jnp.float32) - step_size * m_gate).astype(jnp.bfloat16)
    new_up = (up_local.astype(jnp.float32) - step_size * m_up).astype(jnp.bfloat16)
    totals = (
        lax.psum(new_gate, "replica").astype(jnp.float32),
        lax.psum(new_up, "replica").astype(jnp.float32),
        lax.psum(m_gate.astype(jnp.bfloat16), "replica").astype(jnp.float32),
        lax.psum(m_up.astype(jnp.bfloat16), "replica").astype(jnp.float32),
    )
    replicas = lax.axis_size("replica")
    averaged = [(total / replicas).astype(jnp.bfloat16)[None] for total in totals]
    partial_value = back_rows(d_gate, d_up, gate_local, up_local).reshape(
        experts, capacity, full_width
    )
    summed = lax.psum_scatter(partial_value, "split", scatter_dimension=2, tiled=True).astype(
        jnp.bfloat16
    )
    returned = lax.all_to_all(summed, "expert", split_axis=0, concat_axis=0, tiled=True)
    picked = returned.reshape(experts * capacity, returned.shape[2])[targets]
    d_toks = (
        picked.reshape(tok_count, 2, picked.shape[1])
        .astype(jnp.float32)
        .sum(axis=1)
        .astype(jnp.bfloat16)
    )
    return (averaged[0], averaged[1], averaged[2], averaged[3], d_toks[None])


def solution(mesh):
    return jax.shard_map(
        per_device,
        mesh=mesh,
        in_specs=(
            P("replica", "expert", "split"),
            P("replica", "expert", "split"),
            P("replica", "expert", None),
            P("replica", "expert", None),
            P("replica", "expert", None, "split"),
            P("replica", "expert", None, "split"),
            P("replica", "expert", "split", None),
            P("replica", "expert", None, "split"),
            P("replica", "expert", None, "split"),
        ),
        out_specs=(
            P("expert", None, "split"),
            P("expert", None, "split"),
            P("expert", None, "split"),
            P("expert", None, "split"),
            P("replica", "expert", "split"),
        ),
        check_vma=False,
    )
```

profile of v0, /device:TPU:0, one launch (start us, length us, event | category | flops | bytes accessed | tf_op | source)
XLA Modules:
  0.0 374.2 jit_solution(933145666004161640)
XLA Ops:
  7.2 0.9 copy.15
  8.4 0.7 broadcast_multiply_fusion
  9.1 1.1 reduce-window.6
  10.8 1.6 broadcast_in_dim.26
  12.4 1.2 reshape.123
  13.7 3.9 %scatter_custom_fusion = bf16[1024,1024]{1,0:T(8,128)(2,1)S(1)} fusion(s32[512]{0:T(512)S(1)} %bitcast.63, bf16[512,1024]{1,0:T(8,128)(2,1)} %reshape.123, bf16[]{:T(256)} %constant.10.clone.1), kind=kCustom, calls=%fused_computation.34 | custom fusion | bytes 2097664 | tf_op jit(solution)/shard_map/scatter | solution.py:61
  17.6 55.4 %all_to_all.15 = bf16[8,128,1024]{2,1,0:T(8,128)(2,1)} all-to-all(bf16[8,128,1024]{2,1,0:T(8,128)(2,1)S(1)} %bitcast.60), channel_id=1, replica_groups=mesh['expert'=8,'split'=2,'replica'=2] {'expert'}, dimensions={0} | all-to-all | bytes 4194304 | tf_op jit(solution)/shard_map/all_to_all | solution.py:64
  73.1 1.0 copy-done.6
  74.1 2.1 mul.79
  76.2 2.7 mul.80
  79.2 4.2 %scatter_custom_fusion.1 = bf16[1024,1024]{1,0:T(8,128)(2,1)} fusion(s32[512]{0:T(512)S(1)} %bitcast.64, f32[512,1024]{1,0:T(8,128)S(1)} %mul.80, f32[512]{0:T(512)S(1)} %mul.81, bf16[]{:T(256)} %constant.10.clone.1), kind=kCustom, calls=%fused_computation.17 | custom fusion | flops 1048576 | bytes 4196354 | tf_op jit(solution)/shard_map/scatter | solution.py:62
  83.4 51.8 %all_to_all.16 = bf16[8,128,1024]{2,1,0:T(8,128)(2,1)} all-to-all(bf16[8,128,1024]{2,1,0:T(8,128)(2,1)} %bitcast.59), channel_id=1, replica_groups=mesh['expert'=8,'split'=2,'replica'=2] {'expert'}, dimensions={0} | all-to-all | bytes 4194304 | tf_op jit(solution)/shard_map/all_to_all | solution.py:65
  135.5 0.9 copy-done.2
  136.5 4.4 %fusion.14 = f32[1024,256]{1,0:T(8,128)} fusion(bf16[1024,2048]{1,0:T(8,128)(2,1)} %bitcast.67, bf16[1,1,2048,256]{3,2,1,0:T(8,128)(2,1)S(1)} %copy-done.2), kind=kOutput, calls=%fused_computation.28 | convolution fusion | flops 1073741824 | bytes 6291456 | tf_op jit(solution)/shard_map/dot_general | solution.py:18
  140.9 50.2 %all-gather.5.cloned.1.call-done = bf16[8,128,2048]{2,1,0:T(8,128)(2,1)} async-done(((bf16[8,128,1024]{2,1,0:T(8,128)(2,1)}), bf16[8,128,2048]{2,1,0:T(8,128)(2,1)}) %all-gather.5.cloned.1.call-update) | async-done | bytes 4194320 | tf_op jit(solution)/shard_map/all_gather | solution.py:69
  191.1 4.0 %multiply_convert_fusion.6 = (bf16[1024,256]{1,0:T(8,128)(2,1)S(1)}, f32[1024,256]{1,0:T(8,128)S(1)}) fusion(f32[1024,256]{1,0:T(8,128)} %fusion.14, bf16[1024,2048]{1,0:T(8,128)(2,1)} %bitcast.71, bf16[1,1,256,2048]{3,2,1,0:T(8,128)(2,1)S(1)} %copy-done), kind=kOutput, calls=%fused_computation.30 | convolution fusion | flops 1075314688 | bytes 7864320 | tf_op jit(solution)/shard_map/dot_general | solution.py:22
  195.2 0.3 copy-done.13
  195.5 1.5 fusion.2
  197.0 1.3 fusion.12
  198.3 4.5 %convolution_add_fusion = f32[1024,2048]{1,0:T(8,128)} fusion(f32[1024,2048]{1,0:T(8,128)S(1)} %fusion.12, bf16[1024,256]{1,0:T(8,128)(2,1)S(1)} %get-tuple-element.13, bf16[1,1,2048,256]{3,2,1,0:T(8,128)(2,1)S(1)} %copy-done.3), kind=kOutput, calls=%fused_computation.3 | convolution fusion | flops 1075838976 | bytes 18350080 | tf_op jit(solution)/shard_map/dot_general | solution.py:42
  202.9 5.6 %fusion.23 = (bf16[2048,256]{1,0:T(8,128)(2,1)}, bf16[2048,256]{1,0:T(8,128)(2,1)}) fusion(bf16[1,1,2048,256]{3,2,1,0:T(8,128)(2,1)S(1)} %copy-done.2, bf16[1024,2048]{1,0:T(8,128)(2,1)} %bitcast.68, bf16[1024,256]{1,0:T(8,128)(2,1)S(1)} %fusion.2, bf16[1,1,2048,256]{3,2,1,0:T(8,128)(2,1)} %param.16), kind=kOutput, calls=%fused_computation.47 | convolution fusion | flops 1077936128 | bytes 8912896 | tf_op jit(solution)/shard_map/dot_general | solution.py:29
  208.5 3.1 fusion.22
  211.5 90.7 %reduce-scatter.2.cloned.1.call-done = f32[8,128,1024]{2,1,0:T(8,128)} async-done(((f32[8,128,2048]{2,1,0:T(8,128)}), f32[8,128,1024]{2,1,0:T(8,128)}) %reduce-scatter.2.cloned.1.call-update) | async-done | bytes 4194320 | tf_op jit(solution)/shard_map/reduce_scatter | solution.py:97
  302.2 3.9 %convert_element_type.103 = bf16[8,128,1024]{2,1,0:T(8,128)(2,1)} convert(f32[8,128,1024]{2,1,0:T(8,128)} %reduce-scatter.2.cloned.1.call-done) | non-fusion elementwise | flops 1048576 | bytes 6291456 | tf_op jit(solution)/shard_map/convert_element_type | solution.py:97
  306.1 5.5 %all-to-all-start.2 = ((bf16[8,128,1024]{2,1,0:T(8,128)(2,1)}), bf16[8,128,1024]{2,1,0:T(8,128)(2,1)S(1)}, u32[]{:S(2)}, u32[]{:S(2)}) async-start(bf16[8,128,1024]{2,1,0:T(8,128)(2,1)} %convert_element_type.103), calls=%async_computation.3 | async-start | bytes 4194304 | tf_op jit(solution)/shard_map/all_to_all | solution.py:100
  311.6 22.8 %all-reduce.3.cloned.1.call-done = (bf16[2048,256]{1,0:T(8,128)(2,1)}, bf16[2048,256]{1,0:T(8,128)(2,1)}, bf16[2048,256]{1,0:T(8,128)(2,1)}, bf16[2048,256]{1,0:T(8,128)(2,1)}) async-done(((bf16[2048,256]{1,0:T(8,128)(2,1)}, bf16[2048,256]{1,0:T(8,128)(2,1)}, bf16[2048,256]{1,0:T(8,128)(2,1)}, bf16[2048,256]{1,0:T(8,128)(2,1)}), (bf16[2048,256]{1,0:T(8,128)(2,1)}, bf16[2048,256]{1,0:T(8,128)(2,1)}, ...) | async-done | bytes 4194320 | tf_op jit(solution)/shard_map/psum | solution.py:87
  334.4 3.4 fusion.6
  337.8 1.8 fusion.4
  339.6 20.2 %all-to-all-done.2 = bf16[8,128,1024]{2,1,0:T(8,128)(2,1)S(1)} async-done(((bf16[8,128,1024]{2,1,0:T(8,128)(2,1)}), bf16[8,128,1024]{2,1,0:T(8,128)(2,1)S(1)}, u32[]{:S(2)}, u32[]{:S(2)}) %all-to-all-start.2) | async-done | bytes 2097184 | tf_op jit(solution)/shard_map/all_to_all | solution.py:100
  359.8 2.8 gather_fusion
  362.6 1.5 reshape.109
  364.0 3.6 reduce_sum.25
  (48 shorter events, 1.9 us)
Async XLA Ops:
  7.2 184.0 %copy-start = (bf16[1,1,256,2048]{3,2,1,0:T(8,128)(2,1)S(1)}, bf16[1,1,256,2048]{3,2,1,0:T(8,128)(2,1)}, u32[]{:S(2)}) copy-start(bf16[1,1,256,2048]{3,2,1,0:T(8,128)(2,1)} %param.15) | copy-start | bytes 3145732
  7.2 128.4 %all-gather.3.cloned.1.call-start = ((), (), s32[]{:S(2)}) async-start(), calls=%async_computation.4 | async-start | bytes 6291456 | tf_op jit(solution)/shard_map/all_gather | solution.py:68
  73.0 1.0 copy-start.6
  73.0 118.1 %all-gather.5.cloned.1.call-start = ((), (), s32[]{:S(2)}) async-start(), calls=%async_computation.5 | async-start | bytes 6291456 | tf_op jit(solution)/shard_map/all_gather | solution.py:69
  76.2 2.7 copy-start.9
  135.3 1.2 copy-start.2
  135.3 166.9 %reduce-scatter.2.cloned.1.call-start = ((), (), s32[]{:S(2)}) async-start(), calls=%async_computation.6 | async-start | bytes 12582912 | tf_op jit(solution)/shard_map/reduce_scatter | solution.py:97
  191.1 4.0 %copy-start.3 = (bf16[1,1,2048,256]{3,2,1,0:T(8,128)(2,1)S(1)}, bf16[1,1,2048,256]{3,2,1,0:T(8,128)(2,1)}, u32[]{:S(2)}) copy-start(bf16[1,1,2048,256]{3,2,1,0:T(8,128)(2,1)} %param.14) | copy-start | bytes 3145732
  191.1 4.1 %copy-start.10 = (bf16[8,128,2048]{2,1,0:T(8,128)(2,1)S(1)}, bf16[8,128,2048]{2,1,0:T(8,128)(2,1)}, u32[]{:S(2)}) copy-start(bf16[8,128,2048]{2,1,0:T(8,128)(2,1)} %all-gather.3.cloned.1.call-done) | copy-start | bytes 12582916
  191.1 4.4 %copy-start.13 = (f32[1024,256]{1,0:T(8,128)S(1)}, f32[1024,256]{1,0:T(8,128)}, u32[]{:S(2)}) copy-start(f32[1024,256]{1,0:T(8,128)} %fusion.14) | copy-start | bytes 3145732
  195.1 3.1 copy-start.7
  202.8 5.7 %copy-start.8 = (bf16[1024,256]{1,0:T(8,128)(2,1)S(1)}, bf16[1024,256]{1,0:T(8,128)(2,1)}, u32[]{:S(2)}) copy-start(bf16[1024,256]{1,0:T(8,128)(2,1)} %copy-done.7) | copy-start | bytes 1572868
  202.8 131.6 %all-reduce.3.cloned.1.call-start = ((), (), s32[]{:S(2)}) async-start(), calls=%async_computation.7 | async-start | bytes 8388608 | tf_op jit(solution)/shard_map/psum | solution.py:87
  202.9 5.6 %copy-start.11 = (bf16[8,128,2048]{2,1,0:T(8,128)(2,1)S(1)}, bf16[8,128,2048]{2,1,0:T(8,128)(2,1)}, u32[]{:S(2)}) copy-start(bf16[8,128,2048]{2,1,0:T(8,128)(2,1)} %all-gather.3.cloned.1.call-done) | copy-start | bytes 12582916
  202.9 5.6 %copy-start.12 = (bf16[1,1,2048,256]{3,2,1,0:T(8,128)(2,1)S(1)}, bf16[1,1,2048,256]{3,2,1,0:T(8,128)(2,1)}, u32[]{:S(2)}) copy-start(bf16[1,1,2048,256]{3,2,1,0:T(8,128)(2,1)} %param.17) | copy-start | bytes 3145732
  306.1 53.7 %all-to-all-start.2 = ((bf16[8,128,1024]{2,1,0:T(8,128)(2,1)}), bf16[8,128,1024]{2,1,0:T(8,128)(2,1)S(1)}, u32[]{:S(2)}, u32[]{:S(2)}) async-start(bf16[8,128,1024]{2,1,0:T(8,128)(2,1)} %convert_element_type.103), calls=%async_computation.3 | async-start | bytes 4194304 | tf_op jit(solution)/shard_map/all_to_all | solution.py:100
  334.4 3.4 copy-start.4
  334.4 3.4 copy-start.5
  359.8 7.8 %copy-start.1 = (bf16[1,1,256,2048]{3,2,1,0:T(8,128)(2,1)S(1)}, bf16[1,1,256,2048]{3,2,1,0:T(8,128)(2,1)}, u32[]{:S(2)}) copy-start(bf16[1,1,256,2048]{3,2,1,0:T(8,128)(2,1)} %param.15) | copy-start | bytes 3145732
Sparse Core Ops, SparseCore 0:
  73.1 55.7 all-gather.2
  135.4 55.6 all-gather.4
  202.9 99.2 reduce-scatter.1
  305.6 28.7 all-reduce.2
where the time goes:
time: 375 us; the launch traced here: 374 us
  waiting for transfers between devices  184 us (49%)
  blocking collectives  107 us (29%)
  matrix products  24.2 us (6%)
  local copies, waits for them, and re-layouts  20 us (5%)
  other arithmetic  18.9 us (5%)
  between operations  14 us (4%)
  starting transfers between devices  5.86 us (2%)
    reduce_scatter x1, waiting for transfers between devices, per_device(): lax.psum_scatter(partial_value, 'split', scatter_dimension=2, tiled=True)  90.7 us
    all_to_all x1, blocking collectives, per_device(): lax.all_to_all(slots_in, 'expert', split_axis=0, concat_axis=0, tiled=True)  55.4 us
    all_to_all x1, blocking collectives, per_device(): lax.all_to_all(slots_out, 'expert', split_axis=0, concat_axis=0, tiled=True)  51.8 us
    all_gather x1, waiting for transfers between devices, per_device(): lax.all_gather(half_out, 'split', axis=2, tiled=True)  50.2 us
    psum x1, waiting for transfers between devices, per_device(): lax.psum(new_gate, 'replica').astype(jnp.float32)  22.8 us
    all_to_all x1, waiting for transfers between devices, per_device(): lax.all_to_all(summed, 'expert', split_axis=0, concat_axis=0, tiled=True)  20.2 us
  transfers between devices with their start and end apart: 5, of which 4 were waited for; matrix products, arithmetic and copies ran while one was open for 8% of the time, Pallas kernels for 0%

commit v1 on v0

v1 whole, which is shorter than its diff:
```python
import functools

import jax
import jax.numpy as jnp
from jax import lax
from jax.experimental import pallas as pl
from jax.experimental.pallas import tpu as pltpu
from jax.sharding import PartitionSpec as P

momentum_decay = 0.9
step_size = 0.005
MESH = pl.DeviceIdType.MESH


def slot_targets(ids_block, experts, capacity):
    flat_ids = ids_block.reshape(-1)
    count = flat_ids.shape[0]
    place = jnp.arange(count, dtype=jnp.int32)
    same = (flat_ids[:, None] == flat_ids[None, :]) & (place[None, :] < place[:, None])
    return flat_ids * capacity + jnp.sum(same.astype(jnp.int32), axis=1)


def greet(axes):
    barrier = pltpu.get_barrier_semaphore()
    total = 0
    for name, size in axes:
        here = lax.axis_index(name)

        def signal(step, carry, name=name, size=size, here=here):
            pl.semaphore_signal(
                barrier, inc=1, device_id={name: lax.rem(here + step, size)}, device_id_type=MESH
            )
            return carry

        lax.fori_loop(1, size, signal, 0)
        total += size - 1
    pl.semaphore_wait(barrier, total)


def remote(src, dst, send, recv, name, to):
    return pltpu.make_async_remote_copy(
        src_ref=src, dst_ref=dst, send_sem=send, recv_sem=recv, device_id={name: to}, device_id_type=MESH
    )


def dispatch_kernel(
    experts, splits, pick_ref, scale_ref, tok_ref, grad_ref, in_ref, out_ref,
    slots, own_sem, send_sem, recv_sem, fsend_sem, frecv_sem,
):
    me = lax.axis_index("expert")
    part = lax.axis_index("split")
    width = tok_ref.shape[1]
    got = (in_ref, out_ref)

    def cols(which):
        return pl.ds(pl.multiple_of(which * width, width), width)

    def make(arr, e):
        source = tok_ref if arr == 0 else grad_ref
        rows = jnp.dot(pick_ref[e], source[...], preferred_element_type=jnp.float32)
        if arr == 1:
            rows = rows * scale_ref[e][:, :1]
        slots[arr, e] = rows.astype(jnp.bfloat16)

    def hop(arr, e, frm):
        return remote(
            slots.at[arr, e], got[arr].at[frm, :, cols(part)], send_sem.at[arr, e], recv_sem.at[arr, frm],
            "expert", e,
        )

    def pass_on(arr, block, s, turn, to, frm):
        return remote(
            block, got[arr].at[s, :, cols(frm)], fsend_sem.at[arr, turn, s], frecv_sem.at[arr, turn, s],
            "split", to,
        )

    def keep(arr):
        return pltpu.make_async_copy(slots.at[arr, me], got[arr].at[me, :, cols(part)], own_sem.at[arr])

    greet((("expert", experts), ("split", splits)))
    for arr in range(2):

        def start(step, carry, arr=arr):
            e = lax.rem(me + step, experts)
            make(arr, e)
            hop(arr, e, me).start()
            return carry

        lax.fori_loop(1, experts, start, 0)
        make(arr, me)
        keep(arr).start()
        for turn in range(1, splits):
            pass_on(arr, slots.at[arr, me], me, turn, lax.rem(part + turn, splits), part).start()
    for arr in range(2):

        def forward(step, carry, arr=arr):
            s = lax.rem(me - step + experts, experts)
            hop(arr, s, s).wait_recv()
            for turn in range(1, splits):
                pass_on(
                    arr, got[arr].at[s, :, cols(part)], s, turn, lax.rem(part + turn, splits), part
                ).start()
            return carry

        lax.fori_loop(1, experts, forward, 0)
    for arr in range(2):

        def finish(step, carry, arr=arr):
            e = lax.rem(me + step, experts)
            hop(arr, e, me).wait_send()
            return carry

        lax.fori_loop(1, experts, finish, 0)
        keep(arr).wait()

        def drain(s, carry, arr=arr):
            for turn in range(1, splits):
                frm = lax.rem(part - turn + splits, splits)
                to = lax.rem(part + turn, splits)
                copy = pass_on(arr, slots.at[arr, s], s, turn, to, frm)
                copy.wait_send()
                copy.wait_recv()
            return carry

        lax.fori_loop(0, experts, drain, 0)


def dispatch(pick, scale, tokens, grads, experts, splits):
    capacity, width = pick.shape[1], tokens.shape[1]
    shape = jax.ShapeDtypeStruct((experts, capacity, splits * width), jnp.bfloat16)
    turns = max(splits, 2)
    return pl.pallas_call(
        functools.partial(dispatch_kernel, experts, splits),
        out_shape=(shape, shape),
        in_specs=[pl.BlockSpec(memory_space=pltpu.VMEM)] * 4,
        out_specs=(pl.BlockSpec(memory_space=pl.ANY), pl.BlockSpec(memory_space=pl.ANY)),
        scratch_shapes=[
            pltpu.VMEM((2, experts, capacity, width), jnp.bfloat16),
            pltpu.SemaphoreType.DMA((2,)),
            pltpu.SemaphoreType.DMA((2, experts)),
            pltpu.SemaphoreType.DMA((2, experts)),
            pltpu.SemaphoreType.DMA((2, turns, experts)),
            pltpu.SemaphoreType.DMA((2, turns, experts)),
        ],
        compiler_params=pltpu.CompilerParams(
            collective_id=0, has_side_effects=True, vmem_limit_bytes=40 << 20
        ),
        name="dispatch",
    )(pick, scale, tokens, grads)


def back_kernel(
    experts, splits, replicas, grads_ref, weights_ref, a_ref, b_ref, c_ref, d_ref,
    home_ref, oa_ref, ob_ref, oc_ref, od_ref,
    away, landed, ready, xsend, xrecv, own_sem, send_sem, recv_sem, rsend, rrecv,
):
    me = lax.axis_index("expert")
    part = lax.axis_index("split")
    copy_of = lax.axis_index("replica")
    width = weights_ref.shape[0] // splits
    stepped = (a_ref, b_ref, c_ref, d_ref)
    others = (oa_ref, ob_ref, oc_ref, od_ref)

    def product(e, which):
        rows = pl.ds(pl.multiple_of(which * width, width), width)
        return lax.dot_general(
            grads_ref[e], weights_ref[rows, :], (((1,), (1,)), ((), ())),
            preferred_element_type=jnp.float32,
        )

    def swap(k, turn):
        return remote(
            stepped[k], others[k].at[turn - 1], rsend.at[k, turn], rrecv.at[k, turn],
            "replica", lax.rem(copy_of + turn, replicas),
        )

    def cross(e, turn):
        return remote(
            away.at[turn, e], landed.at[turn, e], xsend.at[turn, e], xrecv.at[turn, e],
            "split", lax.rem(part + turn, splits),
        )

    def hop(e, frm):
        return remote(ready.at[e], home_ref.at[frm], send_sem.at[e], recv_sem.at[frm], "expert", e)

    greet((("expert", experts), ("split", splits), ("replica", replicas)))

    def first(step, carry):
        e = lax.rem(me + step, experts)
        for turn in range(1, splits):
            away[turn, e] = product(e, lax.rem(part + turn, splits)).astype(jnp.bfloat16)
            cross(e, turn).start()
        return carry

    lax.fori_loop(1, experts + 1, first, 0)
    for k in range(4):
        for turn in range(1, replicas):
            swap(k, turn).start()

    def total(e):
        value = product(e, part)
        for turn in range(1, splits):
            cross(e, turn).wait_recv()
            value = value + landed[turn, e].astype(jnp.float32)
        ready[e] = value.astype(jnp.bfloat16)

    def second(step, carry):
        e = lax.rem(me + step, experts)
        total(e)
        hop(e, me).start()
        return carry

    lax.fori_loop(1, experts, second, 0)
    total(me)
    keep = pltpu.make_async_copy(ready.at[me], home_ref.at[me], own_sem.at[0])
    keep.start()

    def last(step, carry):
        hop(lax.rem(me + step, experts), me).wait_send()
        s = lax.rem(me - step + experts, experts)
        hop(s, s).wait_recv()
        return carry

    lax.fori_loop(1, experts, last, 0)

    def sent(e, carry):
        for turn in range(1, splits):
            cross(e, turn).wait_send()
        return carry

    lax.fori_loop(0, experts, sent, 0)
    keep.wait()
    for k in range(4):
        for turn in range(1, replicas):
            swap(k, turn).wait()


def send_back(grads, weights, stepped, experts, splits, replicas):
    capacity = grads.shape[1]
    width = weights.shape[0] // splits
    turns, copies = max(splits, 2), max(replicas, 2)
    held = jax.ShapeDtypeStruct((copies - 1,) + stepped[0].shape, jnp.bfloat16)
    anywhere = pl.BlockSpec(memory_space=pl.ANY)
    inside = pl.BlockSpec(memory_space=pltpu.VMEM)
    return pl.pallas_call(
        functools.partial(back_kernel, experts, splits, replicas),
        out_shape=(jax.ShapeDtypeStruct((experts, capacity, width), jnp.bfloat16),) + (held,) * 4,
        in_specs=[inside] * 2 + [anywhere] * 4,
        out_specs=(anywhere,) * 5,
        scratch_shapes=[
            pltpu.VMEM((turns, experts, capacity, width), jnp.bfloat16),
            pltpu.VMEM((turns, experts, capacity, width), jnp.bfloat16),
            pltpu.VMEM((experts, capacity, width), jnp.bfloat16),
            pltpu.SemaphoreType.DMA((turns, experts)),
            pltpu.SemaphoreType.DMA((turns, experts)),
            pltpu.SemaphoreType.DMA((1,)),
            pltpu.SemaphoreType.DMA((experts,)),
            pltpu.SemaphoreType.DMA((experts,)),
            pltpu.SemaphoreType.DMA((4, copies)),
            pltpu.SemaphoreType.DMA((4, copies)),
        ],
        compiler_params=pltpu.CompilerParams(
            collective_id=1, has_side_effects=True, vmem_limit_bytes=40 << 20
        ),
        name="send_back",
    )(grads, weights, *stepped)


def hidden_grads(rows_in, rows_out, gate_w, up_w, down_w):
    gate_pre = jnp.dot(rows_in, gate_w, preferred_element_type=jnp.float32)
    up_pre = jnp.dot(rows_in, up_w, preferred_element_type=jnp.float32)
    sigmoid_gate = jax.nn.sigmoid(gate_pre)
    activated = gate_pre * sigmoid_gate
    hidden_grad = lax.dot_general(
        rows_out, down_w, (((1,), (1,)), ((), ())), preferred_element_type=jnp.float32
    )
    d_up = (hidden_grad * activated).astype(jnp.bfloat16)
    d_gate = (hidden_grad * up_pre * sigmoid_gate * (1.0 + gate_pre * (1.0 - sigmoid_gate))).astype(
        jnp.bfloat16
    )
    g_gate = lax.dot_general(
        rows_in, d_gate, (((0,), (0,)), ((), ())), preferred_element_type=jnp.float32
    )
    g_up = lax.dot_general(
        rows_in, d_up, (((0,), (0,)), ((), ())), preferred_element_type=jnp.float32
    )
    return (g_gate, g_up, d_gate, d_up)


def per_device(tokens, grad_out, expert_ids, route_probs, w_gate, w_up, w_down, mom_gate, mom_up):
    experts, splits = lax.axis_size("expert"), lax.axis_size("split")
    replicas = lax.axis_size("replica")
    tok_count = tokens.shape[1]
    capacity = 4 * tok_count // experts
    targets = slot_targets(expert_ids[0], experts, capacity).reshape(tok_count, 2)
    slot = jnp.arange(experts * capacity, dtype=jnp.int32)
    hits = [slot[:, None] == targets[:, k][None, :] for k in range(2)]
    pick = (hits[0] | hits[1]).astype(jnp.bfloat16)
    probs = route_probs[0]
    scale = sum(jnp.sum(jnp.where(hits[k], probs[:, k][None, :], 0.0), axis=1) for k in range(2))
    scale = jnp.broadcast_to(scale.reshape(experts, capacity, 1), (experts, capacity, 128))
    recv_in, recv_out = dispatch(
        pick.reshape(experts, capacity, tok_count), scale, tokens[0], grad_out[0], experts, splits
    )
    row_count = experts * capacity
    full_width = recv_in.shape[2]
    gate_local = w_gate[0, 0]
    up_local = w_up[0, 0]
    g_gate, g_up, d_gate, d_up = hidden_grads(
        recv_in.reshape(row_count, full_width),
        recv_out.reshape(row_count, full_width),
        gate_local,
        up_local,
        w_down[0, 0],
    )
    m_gate = momentum_decay * mom_gate[0, 0].astype(jnp.float32) + g_gate
    m_up = momentum_decay * mom_up[0, 0].astype(jnp.float32) + g_up
    stepped = (
        (gate_local.astype(jnp.float32) - step_size * m_gate).astype(jnp.bfloat16),
        (up_local.astype(jnp.float32) - step_size * m_up).astype(jnp.bfloat16),
        m_gate.astype(jnp.bfloat16),
        m_up.astype(jnp.bfloat16),
    )
    returned, *others = send_back(
        jnp.concatenate([d_gate, d_up], axis=1).reshape(experts, capacity, -1),
        jnp.concatenate([gate_local, up_local], axis=1),
        stepped, experts, splits, replicas,
    )
    averaged = []
    for mine, rest in zip(stepped, others):
        total = mine.astype(jnp.float32)
        for turn in range(replicas - 1):
            total = total + rest[turn].astype(jnp.float32)
        averaged.append((total / replicas).astype(jnp.bfloat16)[None])
    d_toks = lax.dot_general(
        pick, returned.reshape(row_count, -1), (((0,), (0,)), ((), ())),
        preferred_element_type=jnp.float32,
    ).astype(jnp.bfloat16)
    return (averaged[0], averaged[1], averaged[2], averaged[3], d_toks[None])


def solution(mesh):
    return jax.shard_map(
        per_device,
        mesh=mesh,
        in_specs=(
            P("replica", "expert", "split"),
            P("replica", "expert", "split"),
            P("replica", "expert", None),
            P("replica", "expert", None),
            P("replica", "expert", None, "split"),
            P("replica", "expert", None, "split"),
            P("replica", "expert", "split", None),
            P("replica", "expert", None, "split"),
            P("replica", "expert", None, "split"),
        ),
        out_specs=(
            P("expert", None, "split"),
            P("expert", None, "split"),
            P("expert", None, "split"),
            P("expert", None, "split"),
            P("replica", "expert", "split"),
        ),
        check_vma=False,
    )
```

time: 375 us -> 215 us (0.57)
  Pallas kernels: 0 us -> 184 us
  waiting for transfers between devices: 184 us -> 0 us
  blocking collectives: 107 us -> 0 us
  local copies, waits for them, and re-layouts: 20 us -> 5.82 us
  between operations: 14 us -> 0.88 us
  matrix products: 24.2 us -> 12.1 us
  other arithmetic: 18.9 us -> 8.46 us
  starting transfers between devices: 5.86 us -> 0 us
    pallas_call x0 -> x2, Pallas kernels: none -> 184 us  [the longest x1 112 us: dispatch(): pl.pallas_call(functools.partial(dispatch_kernel, experts, splits), out_s...]
    all_to_all x2 -> x0, blocking collectives: 107 us -> none  [the longest x1 55.4 us: per_device(): lax.all_to_all(slots_in, 'expert', split_axis=0, concat_axis=0, tiled=True)]
    reduce_scatter x1 -> x0, waiting for transfers between devices: 90.7 us -> none  [per_device(): lax.psum_scatter(partial_value, 'split', scatter_dimension=2, tiled=True)]
    all_gather x2 -> x0, waiting for transfers between devices: 50.3 us -> none  [the longest x1 50.2 us: per_device(): lax.all_gather(half_out, 'split', axis=2, tiled=True)]
    psum x1 -> x0, waiting for transfers between devices: 22.8 us -> none  [per_device(): lax.psum(new_gate, 'replica').astype(jnp.float32)]
    all_to_all x1 -> x0, waiting for transfers between devices: 20.2 us -> none  [per_device(): lax.all_to_all(summed, 'expert', split_axis=0, concat_axis=0, tiled=True)]
    all_to_all x1 -> x0, starting transfers between devices: 5.51 us -> none  [per_device(): lax.all_to_all(summed, 'expert', split_axis=0, concat_axis=0, tiled=True)]
    mul x5 -> x0, local copies, waits for them, and re-layouts: 5.2 us -> none  [the longest x3 4.92 us: per_device(): grad_out[0][:, None, :].astype(jnp.float32) * weights_route[:, :, None]]
  transfers between devices with their start and end apart: 5 -> 0, of which waited for: 4 -> 0; matrix products, arithmetic and copies ran while one was open for 8% -> 0% of each run, Pallas kernels for 0% -> 0%
where the time goes in v1:
time: 215 us; the launch traced here: 211 us
  Pallas kernels  184 us (86%)
  matrix products  12.1 us (6%)
  other arithmetic  8.46 us (4%)
  local copies, waits for them, and re-layouts  5.82 us (3%)
    pallas_call x1, Pallas kernels, dispatch(): pl.pallas_call(functools.partial(dispatch_kernel, experts, splits), out_s...  112 us
    pallas_call x1, Pallas kernels, send_back(): pl.pallas_call(functools.partial(back_kernel, experts, splits, replicas),...  72.4 us
    broadcast_in_dim x4, other arithmetic, per_device(): averaged.append((total / replicas).astype(jnp.bfloat16)[None])  5.12 us
    dot_general x1, matrix products, hidden_grads(): lax.dot_general(rows_in, d_gate, (((0,), (0,)), ((), ())), preferred_elem...  4.74 us

profile of v1, /device:TPU:0, one launch (start us, length us, event | category | flops | bytes accessed | tf_op | source)
XLA Modules:
  0.0 211.4 jit_solution(8732263892297407604)
XLA Ops:
  0.6 0.0 copy-start
  0.6 0.8 fusion.28
  1.4 0.8 copy.21
  2.3 0.1 eq.73
  2.4 0.3 convert_reduce_fusion
  2.7 0.1 reduce_sum.30
  2.8 0.0 copy-start.6
  2.9 0.2 slice_reduce_fusion.1
  3.1 0.4 select_reduce_fusion
  3.4 0.2 broadcast_in_dim.51.scale_ref
  3.6 0.2 or_convert_fusion.pick_ref
  3.8 0.2 copy-done.6
  4.0 1.5 pad_maximum_fusion.weights_ref
  5.5 0.0 copy-done.3
  5.6 111.8 %dispatch.1 = (bf16[8,128,2048]{2,1,0:T(8,128)(2,1)S(1)}, bf16[8,128,2048]{2,1,0:T(8,128)(2,1)S(1)}) custom-call(bf16[8,128,256]{2,1,0:T(8,128)(2,1)S(1)} %or_convert_fusion.pick_ref, f32[8,128,128]{2,1,0:T(8,128)S(1)} %broadcast_in_dim.51.scale_ref, bf16[256,1024]{1,0:T(8,128)(2,1)S(1)} %bitcast.61, bf16[256,1024]{1,0:T(8,128)(2,1)S(1)} %bitcast.62), custom_call_target="tpu_custom_call" | custom-call | tf_op jit(solution)/shard_map/dispatch/pallas_call | solution.py:132
  117.4 1.3 fusion.24
  118.7 1.4 multiply_convert_fusion
  120.0 0.0 copy-start.9
  120.1 1.5 fusion.10
  121.6 0.0 copy-start.11
  121.6 0.8 copy-done.11
  122.4 1.0 pad_maximum_fusion.1
  123.4 2.3 %copy.23 = bf16[1024,512]{1,0:T(8,128)(2,1)} copy(bf16[1024,512]{0,1:T(8,128)(2,1)} %pad_maximum_fusion.1) | data formatting | bytes 2097152 | tf_op jit(solution)/shard_map/concatenate | solution.py:325
  125.7 4.7 %fusion.27 = (bf16[2048,256]{1,0:T(8,128)(2,1)S(1)}, bf16[2048,256]{1,0:T(8,128)(2,1)S(1)}) fusion(bf16[1,1,2048,256]{3,2,1,0:T(8,128)(2,1)} %param.13, bf16[1024,2048]{1,0:T(8,128)(2,1)} %bitcast.65, bf16[1024,256]{0,1:T(8,128)(2,1)} %copy-done.11, bf16[1,1,2048,256]{3,2,1,0:T(8,128)(2,1)} %param.16), kind=kOutput, calls=%fused_computation.52 | convolution fusion | flops 1077936128 | bytes 8912896 | tf_op jit(solution)/shard_map/dot_general | solution.py:281
  130.5 0.2 copy-done.12
  130.7 1.7 fusion.26
  132.3 72.4 %send_back.1 = (bf16[8,128,1024]{2,1,0:T(8,128)(2,1)S(1)}, bf16[1,2048,256]{2,1,0:T(8,128)(2,1)S(1)}, bf16[1,2048,256]{2,1,0:T(8,128)(2,1)S(1)}, bf16[1,2048,256...) custom-call(bf16[8,128,512]{2,1,0:T(8,128)(2,1)S(1)} %bitcast.60, bf16[2048,512]{1,0:T(8,128)(2,1)S(1)} %pad_maximum_fusion.weights_ref, ...), custom_call_target="tpu_custom_call" | custom-call | tf_op jit(solution)/shard_map/send_back/pallas_call | solution.py:245
  204.7 1.3 fusion.15
  206.0 1.3 fusion.14
  207.3 1.3 fusion.12
  208.5 1.3 fusion.13
  209.8 1.6 fusion.11
  (21 shorter events, 0.1 us)
Async XLA Ops:
  0.6 118.0 %copy-start = (bf16[1,1,256,2048]{3,2,1,0:T(8,128)(2,1)S(1)}, bf16[1,1,256,2048]{3,2,1,0:T(8,128)(2,1)}, u32[]{:S(2)}) copy-start(bf16[1,1,256,2048]{3,2,1,0:T(8,128)(2,1)} %param.15) | copy-start | bytes 3145732
  2.8 1.2 copy-start.6
  4.0 1.5 copy-start.2
  4.0 1.5 copy-start.3
  117.3 2.7 %copy-start.4 = (bf16[8,128,2048]{2,1,0:T(8,128)(2,1)}, bf16[8,128,2048]{2,1,0:T(8,128)(2,1)S(1)}, u32[]{:S(2)}) copy-start(bf16[8,128,2048]{2,1,0:T(8,128)(2,1)S(1)} %get-tuple-element.12) | copy-start | bytes 12582916
  118.7 1.4 copy-start.7
  120.0 1.5 copy-start.9
  121.6 0.8 copy-start.11
  125.7 4.8 %copy-start.5 = (bf16[8,128,2048]{2,1,0:T(8,128)(2,1)S(1)}, bf16[8,128,2048]{2,1,0:T(8,128)(2,1)}, u32[]{:S(2)}) copy-start(bf16[8,128,2048]{2,1,0:T(8,128)(2,1)} %copy-done.4) | copy-start | bytes 12582916
  125.7 4.8 %copy-start.8 = (bf16[1,1,2048,256]{3,2,1,0:T(8,128)(2,1)S(1)}, bf16[1,1,2048,256]{3,2,1,0:T(8,128)(2,1)}, u32[]{:S(2)}) copy-start(bf16[1,1,2048,256]{3,2,1,0:T(8,128)(2,1)} %param.14) | copy-start | bytes 3145732
  125.7 4.8 %copy-start.10 = (bf16[1024,256]{0,1:T(8,128)(2,1)S(1)}, bf16[1024,256]{0,1:T(8,128)(2,1)}, u32[]{:S(2)}) copy-start(bf16[1024,256]{0,1:T(8,128)(2,1)} %copy-done.9) | copy-start | bytes 1572868
  125.7 5.0 %copy-start.12 = (bf16[1,1,2048,256]{3,2,1,0:T(8,128)(2,1)S(1)}, bf16[1,1,2048,256]{3,2,1,0:T(8,128)(2,1)}, u32[]{:S(2)}) copy-start(bf16[1,1,2048,256]{3,2,1,0:T(8,128)(2,1)} %param.17) | copy-start | bytes 3145732
  130.7 1.7 copy-start.1

commit v2 on v1

--- a/solution.py
+++ b/solution.py
@@ -43,110 +43,239 @@
     )
 
 
+def near(half):
+    me = lax.axis_index("expert")
+    base = (me // half) * half
+    return lambda step: base + lax.rem(me - base + step, half)
+
+
 def dispatch_kernel(
-    experts, splits, pick_ref, scale_ref, tok_ref, grad_ref, in_ref, out_ref,
-    slots, own_sem, send_sem, recv_sem, fsend_sem, frecv_sem,
+    experts, splits, place_ref, prob_ref, tok_ref, grad_ref, down_ref, in_ref, hid_ref,
+    far_place, far_prob, far_tok, far_grad, slots, rows, far_down, term_out, term_in,
+    raw_send, raw_recv, own_sem, send_sem, recv_sem, fsend_sem, frecv_sem,
+    dsend_sem, drecv_sem, tsend_sem, trecv_sem,
 ):
+    half = experts // 2
     me = lax.axis_index("expert")
     part = lax.axis_index("split")
-    width = tok_ref.shape[1]
-    got = (in_ref, out_ref)
+    base = (me // half) * half
+    mine = me - base
+    partner = lax.rem(me + half, experts)
+    count, width = tok_ref.shape
+    capacity = rows.shape[1]
+    turns = range(1, splits)
+    peer = near(half)
 
     def cols(which):
         return pl.ds(pl.multiple_of(which * width, width), width)
 
-    def make(arr, e):
-        source = tok_ref if arr == 0 else grad_ref
-        rows = jnp.dot(pick_ref[e], source[...], preferred_element_type=jnp.float32)
+    def ahead(turn):
+        return lax.rem(part + turn, splits)
+
+    def behind(turn):
+        return lax.rem(part - turn + splits, splits)
+
+    def raw(k):
+        src = (place_ref, prob_ref, tok_ref, grad_ref)[k]
+        dst = (far_place, far_prob, far_tok, far_grad)[k]
+        return remote(src, dst, raw_send.at[k], raw_recv.at[k], "expert", partner)
+
+    def down(turn):
+        return remote(
+            down_ref.at[:, cols(ahead(turn))], far_down.at[turn],
+            dsend_sem.at[turn], drecv_sem.at[turn], "split", ahead(turn),
+        )
+
+    def make(arr, blk, e):
+        place = far_place if blk else place_ref
+        prob = far_prob if blk else prob_ref
+        source = ((tok_ref, far_tok), (grad_ref, far_grad))[arr][blk]
+        slot = lax.broadcasted_iota(jnp.int32, (capacity, count), 0) + e * capacity
+        first, second = slot == place[0:1, :], slot == place[1:2, :]
+        pick = jnp.where(first | second, 1.0, 0.0).astype(jnp.bfloat16)
+        value = jnp.dot(pick, source[...], preferred_element_type=jnp.float32)
         if arr == 1:
-            rows = rows * scale_ref[e][:, :1]
-        slots[arr, e] = rows.astype(jnp.bfloat16)
-
-    def hop(arr, e, frm):
-        return remote(
-            slots.at[arr, e], got[arr].at[frm, :, cols(part)], send_sem.at[arr, e], recv_sem.at[arr, frm],
-            "expert", e,
-        )
-
-    def pass_on(arr, block, s, turn, to, frm):
-        return remote(
-            block, got[arr].at[s, :, cols(frm)], fsend_sem.at[arr, turn, s], frecv_sem.at[arr, turn, s],
-            "split", to,
-        )
-
-    def keep(arr):
-        return pltpu.make_async_copy(slots.at[arr, me], got[arr].at[me, :, cols(part)], own_sem.at[arr])
-
-    greet((("expert", experts), ("split", splits)))
-    for arr in range(2):
-
-        def start(step, carry, arr=arr):
-            e = lax.rem(me + step, experts)
-            make(arr, e)
-            hop(arr, e, me).start()
+            scale = jnp.where(first, prob[0:1, :], 0.0) + jnp.where(second, prob[1:2, :], 0.0)
+            value = value * jnp.sum(scale, axis=1, keepdims=True)
+        return value.astype(jnp.bfloat16)
+
+    def landing(arr, s):
+        return in_ref.at[s, :, cols(part)] if arr == 0 else rows.at[s]
+
+    def hop(arr, blk, e, s):
+        return remote(
+            slots.at[arr, blk, e - base], landing(arr, s), send_sem.at[arr, blk, e - base],
+            recv_sem.at[arr, s], "expert", e,
+        )
+
+    def pass_on(block, s, turn, frm):
+        return remote(
+            block, in_ref.at[s, :, cols(frm)], fsend_sem.at[turn, s], frecv_sem.at[turn, s],
+            "split", ahead(turn),
+        )
+
+    def term(s, turn):
+        return remote(
+            term_out.at[turn, s], term_in.at[turn, s], tsend_sem.at[turn, s], trecv_sem.at[turn, s],
+            "split", behind(turn),
+        )
+
+    def keep(blk, s):
+        return pltpu.make_async_copy(slots.at[0, blk, mine], in_ref.at[s, :, cols(part)], own_sem.at[blk])
+
+    def over(n0, n1, body):
+        def run(i, carry):
+            body(i)
             return carry
 
-        lax.fori_loop(1, experts, start, 0)
-        make(arr, me)
-        keep(arr).start()
-        for turn in range(1, splits):
-            pass_on(arr, slots.at[arr, me], me, turn, lax.rem(part + turn, splits), part).start()
-    for arr in range(2):
-
-        def forward(step, carry, arr=arr):
-            s = lax.rem(me - step + experts, experts)
-            hop(arr, s, s).wait_recv()
-            for turn in range(1, splits):
-                pass_on(
-                    arr, got[arr].at[s, :, cols(part)], s, turn, lax.rem(part + turn, splits), part
-                ).start()
-            return carry
-
-        lax.fori_loop(1, experts, forward, 0)
-    for arr in range(2):
-
-        def finish(step, carry, arr=arr):
-            e = lax.rem(me + step, experts)
-            hop(arr, e, me).wait_send()
-            return carry
-
-        lax.fori_loop(1, experts, finish, 0)
-        keep(arr).wait()
-
-        def drain(s, carry, arr=arr):
-            for turn in range(1, splits):
-                frm = lax.rem(part - turn + splits, splits)
-                to = lax.rem(part + turn, splits)
-                copy = pass_on(arr, slots.at[arr, s], s, turn, to, frm)
-                copy.wait_send()
-                copy.wait_recv()
-            return carry
-
-        lax.fori_loop(0, experts, drain, 0)
-
-
-def dispatch(pick, scale, tokens, grads, experts, splits):
-    capacity, width = pick.shape[1], tokens.shape[1]
-    shape = jax.ShapeDtypeStruct((experts, capacity, splits * width), jnp.bfloat16)
-    turns = max(splits, 2)
+        lax.fori_loop(n0, n1, run, 0)
+
+    def send_rows(arr, blk):
+        s = partner if blk else me
+
+        def one(step):
+            e = peer(step)
+            slots[arr, blk, e - base] = make(arr, blk, e)
+            hop(arr, blk, e, s).start()
+
+        over(1, half, one)
+        if arr == 0:
+            slots[0, blk, mine] = make(0, blk, me)
+            keep(blk, s).start()
+            for turn in turns:
+                pass_on(slots.at[0, blk, mine], s, turn, part).start()
+        else:
+            rows[s] = make(1, blk, me)
+
+    def other(step, blk):
+        e = peer(half - step)
+        return lax.rem(e + half, experts) if blk else e
+
+    def forward(blk):
+        def one(step):
+            s = other(step, blk)
+            hop(0, blk, peer(half - step), s).wait_recv()
+            for turn in turns:
+                pass_on(in_ref.at[s, :, cols(part)], s, turn, part).start()
+
+        over(1, half, one)
+
+    def terms(s):
+        for turn in turns:
+            value = lax.dot_general(
+                rows[s], far_down[turn], (((1,), (1,)), ((), ())), preferred_element_type=jnp.float32
+            )
+            term_out[turn, s] = value.astype(jnp.bfloat16)
+            term(s, turn).start()
+
+    def use(blk):
+        terms(partner if blk else me)
+
+        def one(step):
+            s = other(step, blk)
+            hop(1, blk, peer(half - step), s).wait_recv()
+            terms(s)
+
+        over(1, half, one)
+
+    barrier = pltpu.get_barrier_semaphore()
+    over(1, half, lambda step: pl.semaphore_signal(
+        barrier, inc=1, device_id={"expert": peer(step)}, device_id_type=MESH))
+    pl.semaphore_signal(barrier, inc=1, device_id={"expert": partner}, device_id_type=MESH)
+    for turn in turns:
+        pl.semaphore_signal(barrier, inc=1, device_id={"split": ahead(turn)}, device_id_type=MESH)
+    pl.semaphore_wait(barrier, half - 1 + 1 + splits - 1)
+
+    for k in range(4):
+        raw(k).start()
+    send_rows(0, 0)
+    for turn in turns:
+        down(turn).start()
+    send_rows(1, 0)
+    forward(0)
+    for k in range(3):
+        raw(k).wait_recv()
+    send_rows(0, 1)
+    for turn in turns:
+        down(turn).wait_recv()
+    use(0)
+    raw(3).wait_recv()
+    send_rows(1, 1)
+    forward(1)
+    use(1)
+
+    def finish(s):
+        value = lax.dot_general(
+            rows[s], down_ref[:, cols(part)], (((1,), (1,)), ((), ())),
+            preferred_element_type=jnp.float32,
+        )
+        for turn in turns:
+            copy = term(s, turn)
+            copy.wait_send()
+            copy.wait_recv()
+            value = value + term_in[turn, s].astype(jnp.float32)
+        hid_ref[s] = value
+
+    over(0, experts, finish)
+
+    def drain(s):
+        for turn in turns:
+            copy = pass_on(slots.at[0, 0, 0], s, turn, behind(turn))
+            copy.wait_send()
+            copy.wait_recv()
+
+    over(0, experts, drain)
+    for blk in range(2):
+        for arr in range(2):
+            over(1, half, lambda step: hop(arr, blk, peer(step), me).wait_send())
+        keep(blk, partner if blk else me).wait()
+    for k in range(4):
+        raw(k).wait_send()
+    for turn in turns:
+        down(turn).wait_send()
+
+
+def dispatch(place, probs, tokens, grads, down_w, experts, splits, capacity):
+    count, width = tokens.shape
+    hidden = down_w.shape[0]
+    half, turns = experts // 2, max(splits, 2)
+    bf16, dma = jnp.bfloat16, pltpu.SemaphoreType.DMA
+    inside = pl.BlockSpec(memory_space=pltpu.VMEM)
     return pl.pallas_call(
         functools.partial(dispatch_kernel, experts, splits),
-        out_shape=(shape, shape),
-        in_specs=[pl.BlockSpec(memory_space=pltpu.VMEM)] * 4,
-        out_specs=(pl.BlockSpec(memory_space=pl.ANY), pl.BlockSpec(memory_space=pl.ANY)),
+        out_shape=(
+            jax.ShapeDtypeStruct((experts, capacity, splits * width), bf16),
+            jax.ShapeDtypeStruct((experts, capacity, hidden), jnp.float32),
+        ),
+        in_specs=[inside] * 5,
+        out_specs=(pl.BlockSpec(memory_space=pl.ANY), inside),
         scratch_shapes=[
-            pltpu.VMEM((2, experts, capacity, width), jnp.bfloat16),
-            pltpu.SemaphoreType.DMA((2,)),
-            pltpu.SemaphoreType.DMA((2, experts)),
-            pltpu.SemaphoreType.DMA((2, experts)),
-            pltpu.SemaphoreType.DMA((2, turns, experts)),
-            pltpu.SemaphoreType.DMA((2, turns, experts)),
+            pltpu.VMEM(place.shape, jnp.int32),
+            pltpu.VMEM(probs.shape, jnp.float32),
+            pltpu.VMEM((count, width), bf16),
+            pltpu.VMEM((count, width), bf16),
+            pltpu.VMEM((2, 2, half, capacity, width), bf16),
+            pltpu.VMEM((experts, capacity, width), bf16),
+            pltpu.VMEM((turns, hidden, width), bf16),
+            pltpu.VMEM((turns, experts, capacity, hidden), bf16),
+            pltpu.VMEM((turns, experts, capacity, hidden), bf16),
+            dma((4,)),
+            dma((4,)),
+            dma((2,)),
+            dma((2, 2, half)),
+            dma((2, experts)),
+            dma((turns, experts)),
+            dma((turns, experts)),
+            dma((turns,)),
+            dma((turns,)),
+            dma((turns, experts)),
+            dma((turns, experts)),
         ],
         compiler_params=pltpu.CompilerParams(
             collective_id=0, has_side_effects=True, vmem_limit_bytes=40 << 20
         ),
         name="dispatch",
-    )(pick, scale, tokens, grads)
+    )(place, probs, tokens, grads, down_w)
 
 
 def back_kernel(
@@ -266,14 +395,11 @@
     )(grads, weights, *stepped)
 
 
-def hidden_grads(rows_in, rows_out, gate_w, up_w, down_w):
+def hidden_grads(rows_in, hidden_grad, gate_w, up_w):
     gate_pre = jnp.dot(rows_in, gate_w, preferred_element_type=jnp.float32)
     up_pre = jnp.dot(rows_in, up_w, preferred_element_type=jnp.float32)
     sigmoid_gate = jax.nn.sigmoid(gate_pre)
     activated = gate_pre * sigmoid_gate
-    hidden_grad = lax.dot_general(
-        rows_out, down_w, (((1,), (1,)), ((), ())), preferred_element_type=jnp.float32
-    )
     d_up = (hidden_grad * activated).astype(jnp.bfloat16)
     d_gate = (hidden_grad * up_pre * sigmoid_gate * (1.0 + gate_pre * (1.0 - sigmoid_gate))).astype(
         jnp.bfloat16
@@ -297,10 +423,10 @@
     hits = [slot[:, None] == targets[:, k][None, :] for k in range(2)]
     pick = (hits[0] | hits[1]).astype(jnp.bfloat16)
     probs = route_probs[0]
-    scale = sum(jnp.sum(jnp.where(hits[k], probs[:, k][None, :], 0.0), axis=1) for k in range(2))
-    scale = jnp.broadcast_to(scale.reshape(experts, capacity, 1), (experts, capacity, 128))
-    recv_in, recv_out = dispatch(
-        pick.reshape(experts, capacity, tok_count), scale, tokens[0], grad_out[0], experts, splits
+    place = jnp.pad(targets.T, ((0, 6), (0, 0)))
+    recv_in, hidden_grad = dispatch(
+        place, jnp.pad(probs.T, ((0, 6), (0, 0))), tokens[0], grad_out[0], w_down[0, 0],
+        experts, splits, capacity,
     )
     row_count = experts * capacity
     full_width = recv_in.shape[2]
@@ -308,10 +434,9 @@
     up_local = w_up[0, 0]
     g_gate, g_up, d_gate, d_up = hidden_grads(
         recv_in.reshape(row_count, full_width),
-        recv_out.reshape(row_count, full_width),
+        hidden_grad.reshape(row_count, -1),
         gate_local,
         up_local,
-        w_down[0, 0],
     )
     m_gate = momentum_decay * mom_gate[0, 0].astype(jnp.float32) + g_gate
     m_up = momentum_decay * mom_up[0, 0].astype(jnp.float32) + g_up

time: 215 us -> 179 us (0.83)
  the two profiles are of different devices: /device:TPU:0 before, /device:TPU:11 now
where the time goes in v2:
time: 179 us; the launch traced here: 178 us
  Pallas kernels  148 us (83%)
  matrix products  13.9 us (8%)
  local copies, waits for them, and re-layouts  8.12 us (5%)
  other arithmetic  7.68 us (4%)
    pallas_call x1, Pallas kernels, dispatch(): pl.pallas_call(functools.partial(dispatch_kernel, experts, splits), out_s...  83.7 us
    pallas_call x1, Pallas kernels, send_back(): pl.pallas_call(functools.partial(back_kernel, experts, splits, replicas),...  64.1 us
    dot_general x1, matrix products, hidden_grads(): lax.dot_general(rows_in, d_gate, (((0,), (0,)), ((), ())), preferred_elem...  4.73 us
    dot_general x1, matrix products, hidden_grads(): gate_pre = jnp.dot(rows_in, gate_w, preferred_element_type=jnp.float32)  4.38 us
    unnamed x27, local copies, waits for them, and re-layouts  4.26 us
    broadcast_in_dim x2, other arithmetic, per_device(): averaged.append((total / replicas).astype(jnp.bfloat16)[None])  3.85 us

profile of v2, /device:TPU:11, one launch (start us, length us, event | category | flops | bytes accessed | tf_op | source)
XLA Modules:
  0.0 178.3 jit_solution(14438284237797079052)
XLA Ops:
  0.6 0.7 pad.9.prob_ref
  1.3 0.8 copy.22
  2.1 0.1 eq.45
  2.3 0.3 convert_reduce_fusion
  2.5 0.1 reduce_sum.12
  2.7 0.1 copy.23
  2.8 0.7 bitcast_add_fusion
  3.5 0.0 copy-start.1
  3.5 0.0 copy-start.2
  3.5 1.8 %pad_maximum_fusion.weights_ref = bf16[2048,512]{1,0:T(8,128)(2,1)S(1)} fusion(bf16[2048,256]{1,0:T(8,128)(2,1)} %bitcast.69, bf16[2048,256]{1,0:T(8,128)(2,1)} %bitcast.68), kind=kLoop, calls=%fused_computation.2 | loop fusion | flops 4194304 | bytes 4194304 | tf_op jit(solution)/shard_map/concatenate | solution.py:451
  5.4 0.1 copy-done.1
  5.5 0.2 copy-done.2
  5.6 83.7 %dispatch.1 = (bf16[8,128,2048]{2,1,0:T(8,128)(2,1)S(1)}, f32[8,128,256]{2,1,0:T(8,128)S(1)}) custom-call(s32[8,256]{1,0:T(8,128)S(1)} %pad.8.place_ref, f32[8,256]{1,0:T(8,128)S(1)} %pad.9.prob_ref, bf16[256,1024]{1,0:T(8,128)(2,1)S(1)} %bitcast.61, bf16[256,1024]{1,0:T(8,128)(2,1)S(1)} %bitcast.62, bf16[256,2048]{1,0:T(8,128)(2,1)S(1)} %bitcast.59), custom_call_target="tpu_custom_call" | custom-call | tf_op jit(solution)/shard_map/dispatch/pallas_call | solution.py:244
  89.3 1.9 %copy-done.3 = bf16[8,128,2048]{2,1,0:T(8,128)(2,1)} copy-done((bf16[8,128,2048]{2,1,0:T(8,128)(2,1)}, bf16[8,128,2048]{2,1,0:T(8,128)(2,1)S(1)}, u32[]{:S(2)}) %copy-start.3) | copy-done | bytes 4194328
  91.3 1.3 copy.24
  92.6 4.4 %multiply_convert_fusion = (bf16[1024,256]{0,1:T(8,128)(2,1)S(1)}, f32[1024,256]{0,1:T(8,128)S(1)}) fusion(f32[1024,256]{0,1:T(8,128)} %copy.24, bf16[1024,2048]{1,0:T(8,128)(2,1)} %bitcast.63, bf16[1,1,2048,256]{3,2,1,0:T(8,128)(2,1)} %param.13), kind=kOutput, calls=%fused_computation.30 | convolution fusion | flops 1075314688 | bytes 7864320 | tf_op jit(solution)/shard_map/dot_general | solution.py:399
  97.0 0.0 copy-start.9
  97.0 0.2 copy-done.7
  97.2 1.5 fusion.10
  98.8 0.0 copy-start.11
  98.8 0.8 copy-done.11
  99.6 1.0 pad_maximum_fusion.1
  100.6 1.5 copy.26
  102.1 0.0 copy-start.8
  102.2 0.0 copy-start.12
  102.2 4.7 %fusion.25 = (bf16[2048,256]{1,0:T(8,128)(2,1)S(1)}, bf16[2048,256]{1,0:T(8,128)(2,1)S(1)}) fusion(bf16[1,1,2048,256]{3,2,1,0:T(8,128)(2,1)} %param.13, bf16[1024,2048]{1,0:T(8,128)(2,1)} %bitcast.64, bf16[1024,256]{0,1:T(8,128)(2,1)} %copy-done.11, bf16[1,1,2048,256]{3,2,1,0:T(8,128)(2,1)} %param.16), kind=kOutput, calls=%fused_computation.43 | convolution fusion | flops 1077936128 | bytes 8912896 | tf_op jit(solution)/shard_map/dot_general | solution.py:407
  106.9 0.2 copy-done.12
  107.1 1.7 fusion.24
  108.8 64.1 %send_back.1 = (bf16[8,128,1024]{2,1,0:T(8,128)(2,1)S(1)}, bf16[1,2048,256]{2,1,0:T(8,128)(2,1)S(1)}, bf16[1,2048,256]{2,1,0:T(8,128)(2,1)S(1)}, bf16[1,2048,256...) custom-call(bf16[8,128,512]{2,1,0:T(8,128)(2,1)S(1)} %bitcast.58, bf16[2048,512]{1,0:T(8,128)(2,1)S(1)} %pad_maximum_fusion.weights_ref, ...), custom_call_target="tpu_custom_call" | custom-call | tf_op jit(solution)/shard_map/send_back/pallas_call | solution.py:374
  172.9 1.9 %fusion.12 = (bf16[1,2048,256]{2,1,0:T(8,128)(2,1)}, bf16[1,2048,256]{2,1,0:T(8,128)(2,1)}) fusion(bf16[2048,256]{1,0:T(8,128)(2,1)S(1)} %get-tuple-element.22.a_ref, bf16[1,2048,256]{2,1,0:T(8,128)(2,1)S(1)} %get-tuple-element.14, bf16[1,2048,256]{2,1,0:T(8,128)(2,1)S(1)} %get-tuple-element.16, bf16[2048,256]{1,0:T(8,128)(2,1)S(1)} %get-tuple-element.21.c_ref), kind=kLoop, calls=%fused_computation.23 | loop fusion | flops 5242880 | bytes 6291456 | tf_op jit(solution)/shard_map/broadcast_in_dim | solution.py:459
  174.9 1.9 %fusion.13 = (bf16[1,2048,256]{2,1,0:T(8,128)(2,1)}, bf16[1,2048,256]{2,1,0:T(8,128)(2,1)}) fusion(bf16[2048,256]{1,0:T(8,128)(2,1)S(1)} %get-tuple-element.20.b_ref, bf16[1,2048,256]{2,1,0:T(8,128)(2,1)S(1)} %get-tuple-element.15, bf16[1,2048,256]{2,1,0:T(8,128)(2,1)S(1)} %get-tuple-element.17, bf16[2048,256]{1,0:T(8,128)(2,1)S(1)} %get-tuple-element.19.d_ref), kind=kLoop, calls=%fused_computation.24 | loop fusion | flops 5242880 | bytes 6291456 | tf_op jit(solution)/shard_map/broadcast_in_dim | solution.py:459
  176.8 1.6 fusion.11
  (16 shorter events, 0.0 us)
Async XLA Ops:
  3.5 1.9 %copy-start = (bf16[1,1,256,2048]{3,2,1,0:T(8,128)(2,1)S(1)}, bf16[1,1,256,2048]{3,2,1,0:T(8,128)(2,1)}, u32[]{:S(2)}) copy-start(bf16[1,1,256,2048]{3,2,1,0:T(8,128)(2,1)} %param.15) | copy-start | bytes 3145732
  3.5 2.0 %copy-start.1 = (bf16[1,256,1024]{2,1,0:T(8,128)(2,1)S(1)}, bf16[1,256,1024]{2,1,0:T(8,128)(2,1)}, u32[]{:S(2)}) copy-start(bf16[1,256,1024]{2,1,0:T(8,128)(2,1)} %param.9) | copy-start | bytes 1572868
  3.5 2.1 %copy-start.2 = (bf16[1,256,1024]{2,1,0:T(8,128)(2,1)S(1)}, bf16[1,256,1024]{2,1,0:T(8,128)(2,1)}, u32[]{:S(2)}) copy-start(bf16[1,256,1024]{2,1,0:T(8,128)(2,1)} %param.10) | copy-start | bytes 1572868
  89.3 2.0 %copy-start.3 = (bf16[8,128,2048]{2,1,0:T(8,128)(2,1)}, bf16[8,128,2048]{2,1,0:T(8,128)(2,1)S(1)}, u32[]{:S(2)}) copy-start(bf16[8,128,2048]{2,1,0:T(8,128)(2,1)S(1)} %get-tuple-element.12) | copy-start | bytes 12582916
  92.6 4.4 %copy-start.4 = (bf16[8,128,2048]{2,1,0:T(8,128)(2,1)S(1)}, bf16[8,128,2048]{2,1,0:T(8,128)(2,1)}, u32[]{:S(2)}) copy-start(bf16[8,128,2048]{2,1,0:T(8,128)(2,1)} %copy-done.3) | copy-start | bytes 12582916
  92.6 4.4 %copy-start.6 = (f32[1024,256]{0,1:T(8,128)S(1)}, f32[1024,256]{0,1:T(8,128)}, u32[]{:S(2)}) copy-start(f32[1024,256]{0,1:T(8,128)} %copy.24) | copy-start | bytes 3145732
  92.6 4.7 %copy-start.7 = (bf16[1,1,2048,256]{3,2,1,0:T(8,128)(2,1)S(1)}, bf16[1,1,2048,256]{3,2,1,0:T(8,128)(2,1)}, u32[]{:S(2)}) copy-start(bf16[1,1,2048,256]{3,2,1,0:T(8,128)(2,1)} %param.14) | copy-start | bytes 3145732
  97.0 1.8 %copy-start.9 = (bf16[1024,256]{0,1:T(8,128)(2,1)}, bf16[1024,256]{0,1:T(8,128)(2,1)S(1)}, u32[]{:S(2)}) copy-start(bf16[1024,256]{0,1:T(8,128)(2,1)S(1)} %get-tuple-element.25) | copy-start | bytes 1572868
  98.8 0.8 copy-start.11
  102.1 4.8 %copy-start.5 = (bf16[8,128,2048]{2,1,0:T(8,128)(2,1)S(1)}, bf16[8,128,2048]{2,1,0:T(8,128)(2,1)}, u32[]{:S(2)}) copy-start(bf16[8,128,2048]{2,1,0:T(8,128)(2,1)} %copy-done.3) | copy-start | bytes 12582916
  102.1 4.8 %copy-start.8 = (bf16[1,1,2048,256]{3,2,1,0:T(8,128)(2,1)S(1)}, bf16[1,1,2048,256]{3,2,1,0:T(8,128)(2,1)}, u32[]{:S(2)}) copy-start(bf16[1,1,2048,256]{3,2,1,0:T(8,128)(2,1)} %param.14) | copy-start | bytes 3145732
  102.2 4.8 %copy-start.10 = (bf16[1024,256]{0,1:T(8,128)(2,1)S(1)}, bf16[1024,256]{0,1:T(8,128)(2,1)}, u32[]{:S(2)}) copy-start(bf16[1024,256]{0,1:T(8,128)(2,1)} %copy-done.9) | copy-start | bytes 1572868
  102.2 4.9 %copy-start.12 = (bf16[1,1,2048,256]{3,2,1,0:T(8,128)(2,1)S(1)}, bf16[1,1,2048,256]{3,2,1,0:T(8,128)(2,1)}, u32[]{:S(2)}) copy-start(bf16[1,1,2048,256]{3,2,1,0:T(8,128)(2,1)} %param.17) | copy-start | bytes 3145732

commit v3 on v2

--- a/solution.py
+++ b/solution.py
@@ -50,8 +50,9 @@
 
 
 def dispatch_kernel(
-    experts, splits, place_ref, prob_ref, tok_ref, grad_ref, down_ref, in_ref, hid_ref,
-    far_place, far_prob, far_tok, far_grad, slots, rows, far_down, term_out, term_in,
+    experts, splits, place_ref, prob_ref, tok_ref, grad_ref, down_ref, gate_ref, up_ref,
+    in_ref, dgate_ref, dup_ref,
+    far_place, far_prob, far_tok, far_grad, slots, rows, far_down, term_out, term_in, pre_gate, pre_up,
     raw_send, raw_recv, own_sem, send_sem, recv_sem, fsend_sem, frecv_sem,
     dsend_sem, drecv_sem, tsend_sem, trecv_sem,
 ):
@@ -199,10 +200,20 @@
     for turn in turns:
         down(turn).wait_recv()
     use(0)
+    def project(s):
+        for turn in turns:
+            pass_on(slots.at[0, 0, 0], s, turn, behind(turn)).wait_recv()
+        pre_gate[s] = jnp.dot(in_ref[s], gate_ref[...], preferred_element_type=jnp.float32)
+        pre_up[s] = jnp.dot(in_ref[s], up_ref[...], preferred_element_type=jnp.float32)
+
     raw(3).wait_recv()
     send_rows(1, 1)
     forward(1)
+    keep(0, me).wait()
+    over(0, half, lambda step: project(peer(half - step)))
     use(1)
+    keep(1, partner).wait()
+    over(0, half, lambda step: project(lax.rem(peer(half - step) + half, experts)))
 
     def finish(s):
         value = lax.dot_general(
@@ -210,32 +221,33 @@
             preferred_element_type=jnp.float32,
         )
         for turn in turns:
-            copy = term(s, turn)
-            copy.wait_send()
-            copy.wait_recv()
+            term(s, turn).wait_recv()
             value = value + term_in[turn, s].astype(jnp.float32)
-        hid_ref[s] = value
-
-    over(0, experts, finish)
+        gate_pre = pre_gate[s]
+        sigmoid_gate = jax.nn.sigmoid(gate_pre)
+        dup_ref[s] = (value * (gate_pre * sigmoid_gate)).astype(jnp.bfloat16)
+        slope = sigmoid_gate * (1.0 + gate_pre * (1.0 - sigmoid_gate))
+        dgate_ref[s] = (value * pre_up[s] * slope).astype(jnp.bfloat16)
+
+    over(0, half, lambda step: finish(peer(half - step)))
+    over(0, half, lambda step: finish(lax.rem(peer(half - step) + half, experts)))
 
     def drain(s):
         for turn in turns:
-            copy = pass_on(slots.at[0, 0, 0], s, turn, behind(turn))
-            copy.wait_send()
-            copy.wait_recv()
+            term(s, turn).wait_send()
+            pass_on(slots.at[0, 0, 0], s, turn, behind(turn)).wait_send()
 
     over(0, experts, drain)
     for blk in range(2):
         for arr in range(2):
             over(1, half, lambda step: hop(arr, blk, peer(step), me).wait_send())
-        keep(blk, partner if blk else me).wait()
     for k in range(4):
         raw(k).wait_send()
     for turn in turns:
         down(turn).wait_send()
 
 
-def dispatch(place, probs, tokens, grads, down_w, experts, splits, capacity):
+def dispatch(place, probs, tokens, grads, down_w, gate_w, up_w, experts, splits, capacity):
     count, width = tokens.shape
     hidden = down_w.shape[0]
     half, turns = experts // 2, max(splits, 2)
@@ -245,10 +257,11 @@
         functools.partial(dispatch_kernel, experts, splits),
         out_shape=(
             jax.ShapeDtypeStruct((experts, capacity, splits * width), bf16),
-            jax.ShapeDtypeStruct((experts, capacity, hidden), jnp.float32),
+            jax.ShapeDtypeStruct((experts, capacity, hidden), bf16),
+            jax.ShapeDtypeStruct((experts, capacity, hidden), bf16),
         ),
-        in_specs=[inside] * 5,
-        out_specs=(pl.BlockSpec(memory_space=pl.ANY), inside),
+        in_specs=[inside] * 7,
+        out_specs=(inside,) * 3,
         scratch_shapes=[
             pltpu.VMEM(place.shape, jnp.int32),
             pltpu.VMEM(probs.shape, jnp.float32),
@@ -259,6 +272,8 @@
             pltpu.VMEM((turns, hidden, width), bf16),
             pltpu.VMEM((turns, experts, capacity, hidden), bf16),
             pltpu.VMEM((turns, experts, capacity, hidden), bf16),
+            pltpu.VMEM((experts, capacity, hidden), jnp.float32),
+            pltpu.VMEM((experts, capacity, hidden), jnp.float32),
             dma((4,)),
             dma((4,)),
             dma((2,)),
@@ -275,27 +290,27 @@
             collective_id=0, has_side_effects=True, vmem_limit_bytes=40 << 20
         ),
         name="dispatch",
-    )(place, probs, tokens, grads, down_w)
+    )(place, probs, tokens, grads, down_w, gate_w, up_w)
 
 
 def back_kernel(
-    experts, splits, replicas, grads_ref, weights_ref, a_ref, b_ref, c_ref, d_ref,
+    experts, splits, replicas, dgate_ref, dup_ref, gate_ref, up_ref, a_ref, b_ref, c_ref, d_ref,
     home_ref, oa_ref, ob_ref, oc_ref, od_ref,
     away, landed, ready, xsend, xrecv, own_sem, send_sem, recv_sem, rsend, rrecv,
 ):
     me = lax.axis_index("expert")
     part = lax.axis_index("split")
     copy_of = lax.axis_index("replica")
-    width = weights_ref.shape[0] // splits
+    width = gate_ref.shape[0] // splits
     stepped = (a_ref, b_ref, c_ref, d_ref)
     others = (oa_ref, ob_ref, oc_ref, od_ref)
 
     def product(e, which):
         rows = pl.ds(pl.multiple_of(which * width, width), width)
+        dims = (((1,), (1,)), ((), ()))
         return lax.dot_general(
-            grads_ref[e], weights_ref[rows, :], (((1,), (1,)), ((), ())),
-            preferred_element_type=jnp.float32,
-        )
+            dgate_ref[e], gate_ref[rows, :], dims, preferred_element_type=jnp.float32
+        ) + lax.dot_general(dup_ref[e], up_ref[rows, :], dims, preferred_element_type=jnp.float32)
 
     def swap(k, turn):
         return remote(
@@ -364,9 +379,9 @@
             swap(k, turn).wait()
 
 
-def send_back(grads, weights, stepped, experts, splits, replicas):
-    capacity = grads.shape[1]
-    width = weights.shape[0] // splits
+def send_back(d_gate, d_up, gate_w, up_w, stepped, experts, splits, replicas):
+    capacity = d_gate.shape[1]
+    width = gate_w.shape[0] // splits
     turns, copies = max(splits, 2), max(replicas, 2)
     held = jax.ShapeDtypeStruct((copies - 1,) + stepped[0].shape, jnp.bfloat16)
     anywhere = pl.BlockSpec(memory_space=pl.ANY)
@@ -374,7 +389,7 @@
     return pl.pallas_call(
         functools.partial(back_kernel, experts, splits, replicas),
         out_shape=(jax.ShapeDtypeStruct((experts, capacity, width), jnp.bfloat16),) + (held,) * 4,
-        in_specs=[inside] * 2 + [anywhere] * 4,
+        in_specs=[inside] * 4 + [anywhere] * 4,
         out_specs=(anywhere,) * 5,
         scratch_shapes=[
             pltpu.VMEM((turns, experts, capacity, width), jnp.bfloat16),
@@ -392,25 +407,7 @@
             collective_id=1, has_side_effects=True, vmem_limit_bytes=40 << 20
         ),
         name="send_back",
-    )(grads, weights, *stepped)
-
-
-def hidden_grads(rows_in, hidden_grad, gate_w, up_w):
-    gate_pre = jnp.dot(rows_in, gate_w, preferred_element_type=jnp.float32)
-    up_pre = jnp.dot(rows_in, up_w, preferred_element_type=jnp.float32)
-    sigmoid_gate = jax.nn.sigmoid(gate_pre)
-    activated = gate_pre * sigmoid_gate
-    d_up = (hidden_grad * activated).astype(jnp.bfloat16)
-    d_gate = (hidden_grad * up_pre * sigmoid_gate * (1.0 + gate_pre * (1.0 - sigmoid_gate))).astype(
-        jnp.bfloat16
-    )
-    g_gate = lax.dot_general(
-        rows_in, d_gate, (((0,), (0,)), ((), ())), preferred_element_type=jnp.float32
-    )
-    g_up = lax.dot_general(
-        rows_in, d_up, (((0,), (0,)), ((), ())), preferred_element_type=jnp.float32
-    )
-    return (g_gate, g_up, d_gate, d_up)
+    )(d_gate, d_up, gate_w, up_w, *stepped)
 
 
 def per_device(tokens, grad_out, expert_ids, route_probs, w_gate, w_up, w_down, mom_gate, mom_up):
@@ -424,19 +421,20 @@
     pick = (hits[0] | hits[1]).astype(jnp.bfloat16)
     probs = route_probs[0]
     place = jnp.pad(targets.T, ((0, 6), (0, 0)))
-    recv_in, hidden_grad = dispatch(
-        place, jnp.pad(probs.T, ((0, 6), (0, 0))), tokens[0], grad_out[0], w_down[0, 0],
-        experts, splits, capacity,
-    )
-    row_count = experts * capacity
-    full_width = recv_in.shape[2]
     gate_local = w_gate[0, 0]
     up_local = w_up[0, 0]
-    g_gate, g_up, d_gate, d_up = hidden_grads(
-        recv_in.reshape(row_count, full_width),
-        hidden_grad.reshape(row_count, -1),
-        gate_local,
-        up_local,
+    recv_in, d_gate, d_up = dispatch(
+        place, jnp.pad(probs.T, ((0, 6), (0, 0))), tokens[0], grad_out[0], w_down[0, 0],
+        gate_local, up_local, experts, splits, capacity,
+    )
+    row_count = experts * capacity
+    dims = (((0,), (0,)), ((), ()))
+    rows_in = recv_in.reshape(row_count, -1)
+    g_gate = lax.dot_general(
+        rows_in, d_gate.reshape(row_count, -1), dims, preferred_element_type=jnp.float32
+    )
+    g_up = lax.dot_general(
+        rows_in, d_up.reshape(row_count, -1), dims, preferred_element_type=jnp.float32
     )
     m_gate = momentum_decay * mom_gate[0, 0].astype(jnp.float32) + g_gate
     m_up = momentum_decay * mom_up[0, 0].astype(jnp.float32) + g_up
@@ -447,8 +445,7 @@
         m_up.astype(jnp.bfloat16),
     )
     returned, *others = send_back(
-        jnp.concatenate([d_gate, d_up], axis=1).reshape(experts, capacity, -1),
-        jnp.concatenate([gate_local, up_local], axis=1),
+        d_gate, d_up, gate_local, up_local,
         stepped, experts, splits, replicas,
     )
     averaged = []

time: 179 us -> 165 us (0.922)
  the two profiles are of different devices: /device:TPU:11 before, /device:TPU:26 now
where the time goes in v3:
time: 165 us
  Pallas kernels  147 us (89%)
  local copies, waits for them, and re-layouts  7.64 us (5%)
  matrix products  4.94 us (3%)
  other arithmetic  4.81 us (3%)
    pallas_call x1, Pallas kernels, dispatch(): pl.pallas_call(functools.partial(dispatch_kernel, experts, splits), out_s...  80.9 us
    pallas_call x1, Pallas kernels, send_back(): pl.pallas_call(functools.partial(back_kernel, experts, splits, replicas),...  65.8 us
    unnamed x19, local copies, waits for them, and re-layouts  6.58 us
    broadcast_in_dim x2, other arithmetic, per_device(): averaged.append((total / replicas).astype(jnp.bfloat16)[None])  3.85 us

profile of v3, /device:TPU:26, one launch (start us, length us, event | category | flops | bytes accessed | tf_op | source)
XLA Modules:
  0.0 164.8 jit_solution(8031883829981707838)
XLA Ops:
  0.6 0.7 pad.9.prob_ref
  1.3 0.8 copy.20
  2.1 0.1 eq.45
  2.3 0.3 convert_reduce_fusion
  2.5 0.1 reduce_sum.12
  2.7 0.1 copy.21
  2.8 0.7 bitcast_add_fusion
  3.5 0.0 copy-start
  3.5 1.2 copy-done
  4.7 0.0 copy-start.2
  4.7 1.2 copy-done.2
  5.9 0.0 copy-start.4
  5.9 1.2 copy-done.4
  7.2 0.0 copy-start.5
  7.2 1.0 copy-done.5
  8.2 0.0 copy-start.6
  8.2 1.0 copy-done.6
  9.2 0.0 copy-start.7
  9.2 80.9 %dispatch.1 = (bf16[8,128,2048]{2,1,0:T(8,128)(2,1)S(1)}, bf16[8,128,256]{2,1,0:T(8,128)(2,1)S(1)}, bf16[8,128,256]{2,1,0:T(8,128)(2,1)S(1)}) custom-call(s32[8,256]{1,0:T(8,128)S(1)} %pad.8.place_ref, f32[8,256]{1,0:T(8,128)S(1)} %pad.9.prob_ref, bf16[256,1024]{1,0:T(8,128)(2,1)S(1)} %bitcast.60, bf16[256,1024]{1,0:T(8,128)(2,1)S(1)} %bitcast.61, ...), custom_call_target="tpu_custom_call" | custom-call | tf_op jit(solution)/shard_map/dispatch/pallas_call | solution.py:256
  90.1 0.0 copy-done.7
  90.1 0.0 copy-start.8
  90.1 1.7 %fusion.20 = (bf16[2048,256]{1,0:T(8,128)(2,1)S(1)}, bf16[2048,256]{1,0:T(8,128)(2,1)S(1)}) fusion(bf16[1,1,2048,256]{3,2,1,0:T(8,128)(2,1)S(1)} %copy-done.2, bf16[8,128,2048]{2,1,0:T(8,128)(2,1)S(1)} %get-tuple-element.13, bf16[8,128,256]{2,1,0:T(8,128)(2,1)S(1)} %get-tuple-element.15.dup_ref, bf16[1,1,2048,256]{3,2,1,0:T(8,128)(2,1)S(1)} %copy-done.7), kind=kOutput, calls=%fused_computation.33 | convolution fusion | flops 1077936128 | bytes 8912896 | tf_op jit(solution)/shard_map/dot_general | solution.py:436
  91.8 0.0 copy-done.8
  91.8 0.0 copy-start.1
  91.8 0.0 copy-start.3
  91.8 1.7 %fusion.21 = (bf16[2048,256]{1,0:T(8,128)(2,1)S(1)}, bf16[2048,256]{1,0:T(8,128)(2,1)S(1)}) fusion(bf16[1,1,2048,256]{3,2,1,0:T(8,128)(2,1)S(1)} %copy-done, bf16[8,128,2048]{2,1,0:T(8,128)(2,1)S(1)} %get-tuple-element.13, bf16[8,128,256]{2,1,0:T(8,128)(2,1)S(1)} %get-tuple-element.14.dgate_ref, bf16[1,1,2048,256]{3,2,1,0:T(8,128)(2,1)S(1)} %copy-done.8), kind=kOutput, calls=%fused_computation.34 | convolution fusion | flops 1077936128 | bytes 8912896 | tf_op jit(solution)/shard_map/dot_general | solution.py:433
  93.6 0.0 copy-done.1
  93.6 0.0 copy-done.3
  93.6 65.8 %send_back.1 = (bf16[8,128,1024]{2,1,0:T(8,128)(2,1)S(1)}, bf16[1,2048,256]{2,1,0:T(8,128)(2,1)S(1)}, bf16[1,2048,256]{2,1,0:T(8,128)(2,1)S(1)}, bf16[1,2048,256...) custom-call(bf16[8,128,256]{2,1,0:T(8,128)(2,1)S(1)} %get-tuple-element.14.dgate_ref, ...), custom_call_target="tpu_custom_call" | custom-call | tf_op jit(solution)/shard_map/send_back/pallas_call | solution.py:389
  159.4 1.9 %fusion.11 = (bf16[1,2048,256]{2,1,0:T(8,128)(2,1)}, bf16[1,2048,256]{2,1,0:T(8,128)(2,1)}) fusion(bf16[2048,256]{1,0:T(8,128)(2,1)S(1)} %get-tuple-element.24.a_ref, bf16[1,2048,256]{2,1,0:T(8,128)(2,1)S(1)} %get-tuple-element.16, bf16[1,2048,256]{2,1,0:T(8,128)(2,1)S(1)} %get-tuple-element.18, bf16[2048,256]{1,0:T(8,128)(2,1)S(1)} %get-tuple-element.23.c_ref), kind=kLoop, calls=%fused_computation.20 | loop fusion | flops 5242880 | bytes 6291456 | tf_op jit(solution)/shard_map/broadcast_in_dim | solution.py:456
  161.3 1.9 %fusion.12 = (bf16[1,2048,256]{2,1,0:T(8,128)(2,1)}, bf16[1,2048,256]{2,1,0:T(8,128)(2,1)}) fusion(bf16[2048,256]{1,0:T(8,128)(2,1)S(1)} %get-tuple-element.22.b_ref, bf16[1,2048,256]{2,1,0:T(8,128)(2,1)S(1)} %get-tuple-element.17, bf16[1,2048,256]{2,1,0:T(8,128)(2,1)S(1)} %get-tuple-element.19, bf16[2048,256]{1,0:T(8,128)(2,1)S(1)} %get-tuple-element.21.d_ref), kind=kLoop, calls=%fused_computation.21 | loop fusion | flops 5242880 | bytes 6291456 | tf_op jit(solution)/shard_map/broadcast_in_dim | solution.py:456
  163.2 1.6 fusion.10
  (2 shorter events, 0.0 us)
Async XLA Ops:
  3.5 1.2 copy-start
  4.7 1.2 copy-start.2
  5.9 1.2 copy-start.4
  7.2 1.0 copy-start.5
  8.2 1.0 copy-start.6
  9.2 80.9 %copy-start.7 = (bf16[1,1,2048,256]{3,2,1,0:T(8,128)(2,1)S(1)}, bf16[1,1,2048,256]{3,2,1,0:T(8,128)(2,1)}, u32[]{:S(2)}) copy-start(bf16[1,1,2048,256]{3,2,1,0:T(8,128)(2,1)} %param.17) | copy-start | bytes 3145732
  90.1 1.7 %copy-start.8 = (bf16[1,1,2048,256]{3,2,1,0:T(8,128)(2,1)S(1)}, bf16[1,1,2048,256]{3,2,1,0:T(8,128)(2,1)}, u32[]{:S(2)}) copy-start(bf16[1,1,2048,256]{3,2,1,0:T(8,128)(2,1)} %param.16) | copy-start | bytes 3145732
  91.8 1.8 %copy-start.1 = (bf16[1,1,2048,256]{3,2,1,0:T(8,128)(2,1)S(1)}, bf16[1,1,2048,256]{3,2,1,0:T(8,128)(2,1)}, u32[]{:S(2)}) copy-start(bf16[1,1,2048,256]{3,2,1,0:T(8,128)(2,1)} %param.13) | copy-start | bytes 3145732
  91.8 1.8 %copy-start.3 = (bf16[1,1,2048,256]{3,2,1,0:T(8,128)(2,1)S(1)}, bf16[1,1,2048,256]{3,2,1,0:T(8,128)(2,1)}, u32[]{:S(2)}) copy-start(bf16[1,1,2048,256]{3,2,1,0:T(8,128)(2,1)} %param.14) | copy-start | bytes 3145732

commit v4 on v3

--- a/solution.py
+++ b/solution.py
@@ -50,9 +50,10 @@
 
 
 def dispatch_kernel(
-    experts, splits, place_ref, prob_ref, tok_ref, grad_ref, down_ref, gate_ref, up_ref,
+    experts, splits, place_ref, prob_ref, tok_hbm, grad_hbm, down_hbm, gate_hbm, up_hbm,
     in_ref, dgate_ref, dup_ref,
     far_place, far_prob, far_tok, far_grad, slots, rows, far_down, term_out, term_in, pre_gate, pre_up,
+    tok_ref, grad_ref, down_ref, gate_ref, up_ref, load_sem,
     raw_send, raw_recv, own_sem, send_sem, recv_sem, fsend_sem, frecv_sem,
     dsend_sem, drecv_sem, tsend_sem, trecv_sem,
 ):
@@ -76,14 +77,19 @@
     def behind(turn):
         return lax.rem(part - turn + splits, splits)
 
+    def load(k):
+        src = (tok_hbm, grad_hbm, down_hbm, gate_hbm, up_hbm)[k]
+        dst = (tok_ref, grad_ref, down_ref, gate_ref, up_ref)[k]
+        return pltpu.make_async_copy(src, dst, load_sem.at[k])
+
     def raw(k):
-        src = (place_ref, prob_ref, tok_ref, grad_ref)[k]
+        src = (place_ref, prob_ref, tok_hbm, grad_hbm)[k]
         dst = (far_place, far_prob, far_tok, far_grad)[k]
         return remote(src, dst, raw_send.at[k], raw_recv.at[k], "expert", partner)
 
     def down(turn):
         return remote(
-            down_ref.at[:, cols(ahead(turn))], far_down.at[turn],
+            down_hbm.at[:, cols(ahead(turn))], far_down.at[turn],
             dsend_sem.at[turn], drecv_sem.at[turn], "split", ahead(turn),
         )
 
@@ -179,6 +185,8 @@
 
         over(1, half, one)
 
+    for k in range(5):
+        load(k).start()
     barrier = pltpu.get_barrier_semaphore()
     over(1, half, lambda step: pl.semaphore_signal(
         barrier, inc=1, device_id={"expert": peer(step)}, device_id_type=MESH))
@@ -187,15 +195,18 @@
         pl.semaphore_signal(barrier, inc=1, device_id={"split": ahead(turn)}, device_id_type=MESH)
     pl.semaphore_wait(barrier, half - 1 + 1 + splits - 1)
 
-    for k in range(4):
+    for k in range(3):
         raw(k).start()
+    load(0).wait()
     send_rows(0, 0)
     for turn in turns:
         down(turn).start()
+    load(1).wait()
     send_rows(1, 0)
     forward(0)
     for k in range(3):
         raw(k).wait_recv()
+    raw(3).start()
     send_rows(0, 1)
     for turn in turns:
         down(turn).wait_recv()
@@ -209,6 +220,8 @@
     raw(3).wait_recv()
     send_rows(1, 1)
     forward(1)
+    for k in range(2, 5):
+        load(k).wait()
     keep(0, me).wait()
     over(0, half, lambda step: project(peer(half - step)))
     use(1)
@@ -260,7 +273,7 @@
             jax.ShapeDtypeStruct((experts, capacity, hidden), bf16),
             jax.ShapeDtypeStruct((experts, capacity, hidden), bf16),
         ),
-        in_specs=[inside] * 7,
+        in_specs=[inside] * 2 + [pl.BlockSpec(memory_space=pltpu.HBM)] * 5,
         out_specs=(inside,) * 3,
         scratch_shapes=[
             pltpu.VMEM(place.shape, jnp.int32),
@@ -274,6 +287,12 @@
             pltpu.VMEM((turns, experts, capacity, hidden), bf16),
             pltpu.VMEM((experts, capacity, hidden), jnp.float32),
             pltpu.VMEM((experts, capacity, hidden), jnp.float32),
+            pltpu.VMEM((count, width), bf16),
+            pltpu.VMEM((count, width), bf16),
+            pltpu.VMEM(down_w.shape, bf16),
+            pltpu.VMEM(gate_w.shape, bf16),
+            pltpu.VMEM(up_w.shape, bf16),
+            dma((5,)),
             dma((4,)),
             dma((4,)),
             dma((2,)),
@@ -329,14 +348,22 @@
 
     greet((("expert", experts), ("split", splits), ("replica", replicas)))
 
+    half = experts // 2
+    peer = near(half)
+
+    def order(step):
+        return lax.rem(peer(lax.rem(step, half)) + half * (1 - step // half), experts)
+
     def first(step, carry):
-        e = lax.rem(me + step, experts)
+        e = order(step)
         for turn in range(1, splits):
             away[turn, e] = product(e, lax.rem(part + turn, splits)).astype(jnp.bfloat16)
             cross(e, turn).start()
         return carry
 
-    lax.fori_loop(1, experts + 1, first, 0)
+    lax.fori_loop(0, half, first, 0)
+    lax.fori_loop(half + 1, experts, first, 0)
+    first(half, 0)
     for k in range(4):
         for turn in range(1, replicas):
             swap(k, turn).start()
@@ -349,12 +376,13 @@
         ready[e] = value.astype(jnp.bfloat16)
 
     def second(step, carry):
-        e = lax.rem(me + step, experts)
+        e = order(step)
         total(e)
         hop(e, me).start()
         return carry
 
-    lax.fori_loop(1, experts, second, 0)
+    lax.fori_loop(0, half, second, 0)
+    lax.fori_loop(half + 1, experts, second, 0)
     total(me)
     keep = pltpu.make_async_copy(ready.at[me], home_ref.at[me], own_sem.at[0])
     keep.start()

time: 165 us -> 160 us (0.970)
  the two profiles are of different devices: /device:TPU:26 before, /device:TPU:0 now
where the time goes in v4:
time: 160 us
  Pallas kernels  142 us (89%)
  local copies, waits for them, and re-layouts  7.64 us (5%)
  matrix products  4.94 us (3%)
  other arithmetic  4.81 us (3%)
    pallas_call x1, Pallas kernels, dispatch(): pl.pallas_call(functools.partial(dispatch_kernel, experts, splits), out_s...  84 us
    pallas_call x1, Pallas kernels, send_back(): pl.pallas_call(functools.partial(back_kernel, experts, splits, replicas),...  57.6 us
    unnamed x19, local copies, waits for them, and re-layouts  6.58 us
    broadcast_in_dim x2, other arithmetic, per_device(): averaged.append((total / replicas).astype(jnp.bfloat16)[None])  3.85 us

profile of v4, /device:TPU:0, one launch (start us, length us, event | category | flops | bytes accessed | tf_op | source)
XLA Modules:
  0.0 159.7 jit_solution(6930524154498597458)
XLA Ops:
  0.6 0.7 pad.9.prob_ref
  1.3 0.8 copy.20
  2.1 0.1 eq.45
  2.3 0.3 convert_reduce_fusion
  2.5 0.1 reduce_sum.12
  2.7 0.1 copy.21
  2.8 0.7 bitcast_add_fusion
  3.5 0.0 copy-start
  3.5 1.2 copy-done
  4.7 0.0 copy-start.2
  4.7 1.2 copy-done.2
  5.9 0.0 copy-start.4
  5.9 1.2 copy-done.4
  7.2 0.0 copy-start.5
  7.2 1.0 copy-done.5
  8.2 0.0 copy-start.6
  8.2 1.0 copy-done.6
  9.2 0.0 copy-start.7
  9.2 84.0 %dispatch.1 = (bf16[8,128,2048]{2,1,0:T(8,128)(2,1)S(1)}, bf16[8,128,256]{2,1,0:T(8,128)(2,1)S(1)}, bf16[8,128,256]{2,1,0:T(8,128)(2,1)S(1)}) custom-call(s32[8,256]{1,0:T(8,128)S(1)} %pad.8.place_ref, f32[8,256]{1,0:T(8,128)S(1)} %pad.9.prob_ref, bf16[256,1024]{1,0:T(8,128)(2,1)S(1)} %bitcast.60, bf16[256,1024]{1,0:T(8,128)(2,1)S(1)} %bitcast.61, ...), custom_call_target="tpu_custom_call" | custom-call | tf_op jit(solution)/shard_map/dispatch/pallas_call | solution.py:269
  93.2 0.0 copy-done.7
  93.3 0.0 copy-start.8
  93.3 1.7 %fusion.20 = (bf16[2048,256]{1,0:T(8,128)(2,1)S(1)}, bf16[2048,256]{1,0:T(8,128)(2,1)S(1)}) fusion(bf16[1,1,2048,256]{3,2,1,0:T(8,128)(2,1)S(1)} %copy-done.2, bf16[8,128,2048]{2,1,0:T(8,128)(2,1)S(1)} %get-tuple-element.13, bf16[8,128,256]{2,1,0:T(8,128)(2,1)S(1)} %get-tuple-element.15.dup_ref, bf16[1,1,2048,256]{3,2,1,0:T(8,128)(2,1)S(1)} %copy-done.7), kind=kOutput, calls=%fused_computation.33 | convolution fusion | flops 1077936128 | bytes 8912896 | tf_op jit(solution)/shard_map/dot_general | solution.py:464
  94.9 0.0 copy-done.8
  95.0 0.0 copy-start.1
  95.0 0.0 copy-start.3
  95.0 1.7 %fusion.21 = (bf16[2048,256]{1,0:T(8,128)(2,1)S(1)}, bf16[2048,256]{1,0:T(8,128)(2,1)S(1)}) fusion(bf16[1,1,2048,256]{3,2,1,0:T(8,128)(2,1)S(1)} %copy-done, bf16[8,128,2048]{2,1,0:T(8,128)(2,1)S(1)} %get-tuple-element.13, bf16[8,128,256]{2,1,0:T(8,128)(2,1)S(1)} %get-tuple-element.14.dgate_ref, bf16[1,1,2048,256]{3,2,1,0:T(8,128)(2,1)S(1)} %copy-done.8), kind=kOutput, calls=%fused_computation.34 | convolution fusion | flops 1077936128 | bytes 8912896 | tf_op jit(solution)/shard_map/dot_general | solution.py:461
  96.7 0.0 copy-done.1
  96.7 0.0 copy-done.3
  96.7 57.6 %send_back.1 = (bf16[8,128,1024]{2,1,0:T(8,128)(2,1)S(1)}, bf16[1,2048,256]{2,1,0:T(8,128)(2,1)S(1)}, bf16[1,2048,256]{2,1,0:T(8,128)(2,1)S(1)}, bf16[1,2048,256...) custom-call(bf16[8,128,256]{2,1,0:T(8,128)(2,1)S(1)} %get-tuple-element.14.dgate_ref, ...), custom_call_target="tpu_custom_call" | custom-call | tf_op jit(solution)/shard_map/send_back/pallas_call | solution.py:417
  154.3 1.9 %fusion.11 = (bf16[1,2048,256]{2,1,0:T(8,128)(2,1)}, bf16[1,2048,256]{2,1,0:T(8,128)(2,1)}) fusion(bf16[2048,256]{1,0:T(8,128)(2,1)S(1)} %get-tuple-element.24.a_ref, bf16[1,2048,256]{2,1,0:T(8,128)(2,1)S(1)} %get-tuple-element.16, bf16[1,2048,256]{2,1,0:T(8,128)(2,1)S(1)} %get-tuple-element.18, bf16[2048,256]{1,0:T(8,128)(2,1)S(1)} %get-tuple-element.23.c_ref), kind=kLoop, calls=%fused_computation.20 | loop fusion | flops 5242880 | bytes 6291456 | tf_op jit(solution)/shard_map/broadcast_in_dim | solution.py:484
  156.2 1.9 %fusion.12 = (bf16[1,2048,256]{2,1,0:T(8,128)(2,1)}, bf16[1,2048,256]{2,1,0:T(8,128)(2,1)}) fusion(bf16[2048,256]{1,0:T(8,128)(2,1)S(1)} %get-tuple-element.22.b_ref, bf16[1,2048,256]{2,1,0:T(8,128)(2,1)S(1)} %get-tuple-element.17, bf16[1,2048,256]{2,1,0:T(8,128)(2,1)S(1)} %get-tuple-element.19, bf16[2048,256]{1,0:T(8,128)(2,1)S(1)} %get-tuple-element.21.d_ref), kind=kLoop, calls=%fused_computation.21 | loop fusion | flops 5242880 | bytes 6291456 | tf_op jit(solution)/shard_map/broadcast_in_dim | solution.py:484
  158.2 1.6 fusion.10
  (2 shorter events, 0.0 us)
Async XLA Ops:
  3.5 1.2 copy-start
  4.7 1.2 copy-start.2
  5.9 1.2 copy-start.4
  7.2 1.0 copy-start.5
  8.2 1.0 copy-start.6
  9.2 84.0 %copy-start.7 = (bf16[1,1,2048,256]{3,2,1,0:T(8,128)(2,1)S(1)}, bf16[1,1,2048,256]{3,2,1,0:T(8,128)(2,1)}, u32[]{:S(2)}) copy-start(bf16[1,1,2048,256]{3,2,1,0:T(8,128)(2,1)} %param.17) | copy-start | bytes 3145732
  93.3 1.7 %copy-start.8 = (bf16[1,1,2048,256]{3,2,1,0:T(8,128)(2,1)S(1)}, bf16[1,1,2048,256]{3,2,1,0:T(8,128)(2,1)}, u32[]{:S(2)}) copy-start(bf16[1,1,2048,256]{3,2,1,0:T(8,128)(2,1)} %param.16) | copy-start | bytes 3145732
  95.0 1.8 %copy-start.1 = (bf16[1,1,2048,256]{3,2,1,0:T(8,128)(2,1)S(1)}, bf16[1,1,2048,256]{3,2,1,0:T(8,128)(2,1)}, u32[]{:S(2)}) copy-start(bf16[1,1,2048,256]{3,2,1,0:T(8,128)(2,1)} %param.13) | copy-start | bytes 3145732
  95.0 1.8 %copy-start.3 = (bf16[1,1,2048,256]{3,2,1,0:T(8,128)(2,1)S(1)}, bf16[1,1,2048,256]{3,2,1,0:T(8,128)(2,1)}, u32[]{:S(2)}) copy-start(bf16[1,1,2048,256]{3,2,1,0:T(8,128)(2,1)} %param.14) | copy-start | bytes 3145732

commit v5 on v4

--- a/solution.py
+++ b/solution.py
@@ -201,9 +201,9 @@
     send_rows(0, 0)
     for turn in turns:
         down(turn).start()
+    forward(0)
     load(1).wait()
     send_rows(1, 0)
-    forward(0)
     for k in range(3):
         raw(k).wait_recv()
     raw(3).start()

time: 160 us -> 158 us (0.988)
  Pallas kernels: 142 us -> 140 us
where the time goes in v5:
time: 158 us
  Pallas kernels  140 us (89%)
  local copies, waits for them, and re-layouts  7.64 us (5%)
  matrix products  4.94 us (3%)
  other arithmetic  4.81 us (3%)
    pallas_call x1, Pallas kernels, dispatch(): pl.pallas_call(functools.partial(dispatch_kernel, experts, splits), out_s...  83.5 us
    pallas_call x1, Pallas kernels, send_back(): pl.pallas_call(functools.partial(back_kernel, experts, splits, replicas),...  56.5 us
    unnamed x19, local copies, waits for them, and re-layouts  6.58 us
    broadcast_in_dim x2, other arithmetic, per_device(): averaged.append((total / replicas).astype(jnp.bfloat16)[None])  3.85 us

profile of v5, /device:TPU:0, one launch (start us, length us, event | category | flops | bytes accessed | tf_op | source)
XLA Modules:
  0.0 158.1 jit_solution(10009958245302129738)
XLA Ops:
  0.6 0.7 pad.9.prob_ref
  1.3 0.8 copy.20
  2.1 0.1 eq.45
  2.3 0.3 convert_reduce_fusion
  2.5 0.1 reduce_sum.12
  2.7 0.1 copy.21
  2.8 0.7 bitcast_add_fusion
  3.5 0.0 copy-start
  3.5 1.2 copy-done
  4.7 0.0 copy-start.2
  4.7 1.2 copy-done.2
  5.9 0.0 copy-start.4
  5.9 1.2 copy-done.4
  7.2 0.0 copy-start.5
  7.2 1.0 copy-done.5
  8.2 0.0 copy-start.6
  8.2 1.0 copy-done.6
  9.2 0.0 copy-start.7
  9.2 83.5 %dispatch.1 = (bf16[8,128,2048]{2,1,0:T(8,128)(2,1)S(1)}, bf16[8,128,256]{2,1,0:T(8,128)(2,1)S(1)}, bf16[8,128,256]{2,1,0:T(8,128)(2,1)S(1)}) custom-call(s32[8,256]{1,0:T(8,128)S(1)} %pad.8.place_ref, f32[8,256]{1,0:T(8,128)S(1)} %pad.9.prob_ref, bf16[256,1024]{1,0:T(8,128)(2,1)S(1)} %bitcast.60, bf16[256,1024]{1,0:T(8,128)(2,1)S(1)} %bitcast.61, ...), custom_call_target="tpu_custom_call" | custom-call | tf_op jit(solution)/shard_map/dispatch/pallas_call | solution.py:269
  92.7 0.0 copy-done.7
  92.7 0.0 copy-start.8
  92.7 1.7 %fusion.20 = (bf16[2048,256]{1,0:T(8,128)(2,1)S(1)}, bf16[2048,256]{1,0:T(8,128)(2,1)S(1)}) fusion(bf16[1,1,2048,256]{3,2,1,0:T(8,128)(2,1)S(1)} %copy-done.2, bf16[8,128,2048]{2,1,0:T(8,128)(2,1)S(1)} %get-tuple-element.13, bf16[8,128,256]{2,1,0:T(8,128)(2,1)S(1)} %get-tuple-element.15.dup_ref, bf16[1,1,2048,256]{3,2,1,0:T(8,128)(2,1)S(1)} %copy-done.7), kind=kOutput, calls=%fused_computation.33 | convolution fusion | flops 1077936128 | bytes 8912896 | tf_op jit(solution)/shard_map/dot_general | solution.py:464
  94.4 0.0 copy-done.8
  94.4 0.0 copy-start.1
  94.4 0.0 copy-start.3
  94.4 1.7 %fusion.21 = (bf16[2048,256]{1,0:T(8,128)(2,1)S(1)}, bf16[2048,256]{1,0:T(8,128)(2,1)S(1)}) fusion(bf16[1,1,2048,256]{3,2,1,0:T(8,128)(2,1)S(1)} %copy-done, bf16[8,128,2048]{2,1,0:T(8,128)(2,1)S(1)} %get-tuple-element.13, bf16[8,128,256]{2,1,0:T(8,128)(2,1)S(1)} %get-tuple-element.14.dgate_ref, bf16[1,1,2048,256]{3,2,1,0:T(8,128)(2,1)S(1)} %copy-done.8), kind=kOutput, calls=%fused_computation.34 | convolution fusion | flops 1077936128 | bytes 8912896 | tf_op jit(solution)/shard_map/dot_general | solution.py:461
  96.2 0.0 copy-done.1
  96.2 0.0 copy-done.3
  96.2 56.5 %send_back.1 = (bf16[8,128,1024]{2,1,0:T(8,128)(2,1)S(1)}, bf16[1,2048,256]{2,1,0:T(8,128)(2,1)S(1)}, bf16[1,2048,256]{2,1,0:T(8,128)(2,1)S(1)}, bf16[1,2048,256...) custom-call(bf16[8,128,256]{2,1,0:T(8,128)(2,1)S(1)} %get-tuple-element.14.dgate_ref, ...), custom_call_target="tpu_custom_call" | custom-call | tf_op jit(solution)/shard_map/send_back/pallas_call | solution.py:417
  152.7 1.9 %fusion.11 = (bf16[1,2048,256]{2,1,0:T(8,128)(2,1)}, bf16[1,2048,256]{2,1,0:T(8,128)(2,1)}) fusion(bf16[2048,256]{1,0:T(8,128)(2,1)S(1)} %get-tuple-element.24.a_ref, bf16[1,2048,256]{2,1,0:T(8,128)(2,1)S(1)} %get-tuple-element.16, bf16[1,2048,256]{2,1,0:T(8,128)(2,1)S(1)} %get-tuple-element.18, bf16[2048,256]{1,0:T(8,128)(2,1)S(1)} %get-tuple-element.23.c_ref), kind=kLoop, calls=%fused_computation.20 | loop fusion | flops 5242880 | bytes 6291456 | tf_op jit(solution)/shard_map/broadcast_in_dim | solution.py:484
  154.6 1.9 %fusion.12 = (bf16[1,2048,256]{2,1,0:T(8,128)(2,1)}, bf16[1,2048,256]{2,1,0:T(8,128)(2,1)}) fusion(bf16[2048,256]{1,0:T(8,128)(2,1)S(1)} %get-tuple-element.22.b_ref, bf16[1,2048,256]{2,1,0:T(8,128)(2,1)S(1)} %get-tuple-element.17, bf16[1,2048,256]{2,1,0:T(8,128)(2,1)S(1)} %get-tuple-element.19, bf16[2048,256]{1,0:T(8,128)(2,1)S(1)} %get-tuple-element.21.d_ref), kind=kLoop, calls=%fused_computation.21 | loop fusion | flops 5242880 | bytes 6291456 | tf_op jit(solution)/shard_map/broadcast_in_dim | solution.py:484
  156.5 1.6 fusion.10
  (2 shorter events, 0.0 us)
Async XLA Ops:
  3.5 1.2 copy-start
  4.7 1.2 copy-start.2
  5.9 1.2 copy-start.4
  7.2 1.0 copy-start.5
  8.2 1.0 copy-start.6
  9.2 83.5 %copy-start.7 = (bf16[1,1,2048,256]{3,2,1,0:T(8,128)(2,1)S(1)}, bf16[1,1,2048,256]{3,2,1,0:T(8,128)(2,1)}, u32[]{:S(2)}) copy-start(bf16[1,1,2048,256]{3,2,1,0:T(8,128)(2,1)} %param.17) | copy-start | bytes 3145732
  92.7 1.7 %copy-start.8 = (bf16[1,1,2048,256]{3,2,1,0:T(8,128)(2,1)S(1)}, bf16[1,1,2048,256]{3,2,1,0:T(8,128)(2,1)}, u32[]{:S(2)}) copy-start(bf16[1,1,2048,256]{3,2,1,0:T(8,128)(2,1)} %param.16) | copy-start | bytes 3145732
  94.4 1.8 %copy-start.1 = (bf16[1,1,2048,256]{3,2,1,0:T(8,128)(2,1)S(1)}, bf16[1,1,2048,256]{3,2,1,0:T(8,128)(2,1)}, u32[]{:S(2)}) copy-start(bf16[1,1,2048,256]{3,2,1,0:T(8,128)(2,1)} %param.13) | copy-start | bytes 3145732
  94.4 1.8 %copy-start.3 = (bf16[1,1,2048,256]{3,2,1,0:T(8,128)(2,1)S(1)}, bf16[1,1,2048,256]{3,2,1,0:T(8,128)(2,1)}, u32[]{:S(2)}) copy-start(bf16[1,1,2048,256]{3,2,1,0:T(8,128)(2,1)} %param.14) | copy-start | bytes 3145732
